TPU v7x, 32 devices: a whole 2x2x4 slice. The times are simulated.
32 devices in a mesh: seq: 8 (over y, x, core), chan: 4 (over z).
Axes of the slice: x: 2, y: 2, z: 4, core: 2. Of those that a mesh axis runs over, the one named last changes fastest.
Arguments:
- tokens: bfloat16 [6144, 4096], P('seq', 'chan'), may hold values from -4 to 4
- w_in: bfloat16 [8, 4096, 1296], P('chan', 'seq'), may hold values from -1 to 1
- conv_w: float32 [8, 4, 1280], P('chan'), may hold values from -3 to 3
- conv_b: float32 [8, 1280], P('chan'), may hold values from -3 to 3
- dt_bias: float32 [8, 16], P('chan'), may hold values from -8 to 2
- a_log: float32 [8, 16], P('chan'), may hold values from -4.6 to -3.7
- d_skip: float32 [8, 16], P('chan'), may hold values from 0.3 to 3
- norm_gain: float32 [8, 1024], P('chan'), may hold values from 0.5 to 1.5
Outputs:
- mixer_out: bfloat16 [6144, 8192], P('seq', 'chan')
All inputs are finite; a program needn't handle non-finite values.
Results may differ from a plain program's by a relative error of at most 0.0076.
Values may be sent and summed in bfloat16 or wider, within the bound.
A program may use at most 128 MiB of HBM per device.

v0:
```python
import jax
import jax.numpy as jnp
from jax import lax
from jax.sharding import PartitionSpec as P

P_SIZE = 64
N = 128
KCONV = 4
Q = 128
HG = 16
GW = 1024
CW = 1280


epsilon = 1e-05


def shifted(block, axis, distance):
    devices = range(lax.axis_size(axis))
    route = [(i - distance, i) for i in devices if i - distance in devices]
    return lax.ppermute(block, axis, route)


def entering(part, axis, combine, identity):
    place = lax.axis_index(axis)
    gathered = jax.tree.map(lambda a: lax.all_gather(a, axis), part)
    state = jax.tree.map(lambda a, e: jnp.zeros_like(a) + jnp.asarray(e, a.dtype), part, identity)

    def one(step, state):
        return combine(
            state, jax.tree.map(lambda a: lax.dynamic_index_in_dim(a, step, 0, False), gathered)
        )

    return lax.fori_loop(0, place, one, state)


def combine_states(earlier, later_one):
    return (earlier[0] * later_one[0], later_one[0][..., None, None] * earlier[1] + later_one[1])


def mix_groups(gathered, w_in, conv_w, conv_b, dt_bias, a_log, d_skip, norm_gain):
    groups = w_in.shape[0]
    row_count = gathered.shape[0]
    projected = jnp.einsum(
        "td,gdc->tgc",
        gathered,
        lax.all_gather(w_in, "seq", axis=1, tiled=True),
        preferred_element_type=jnp.float32,
    )
    conv_in = projected[:, :, :CW].astype(jnp.bfloat16)
    raw_dt = projected[gathered.shape[0] - row_count :, :, CW:]
    rim_rows = shifted(conv_in[row_count - (KCONV - 1) :], "seq", 1)
    padded = jnp.concatenate([rim_rows, conv_in], axis=0)
    pre_act = jnp.broadcast_to(conv_b[None], (row_count, groups, CW))
    for offset in range(KCONV):
        pre_act = pre_act + conv_w[None, :, offset] * padded[offset : offset + row_count]
    inputs = jax.nn.silu(pre_act).astype(jnp.bfloat16)
    block_count = row_count // Q
    blocked = inputs.reshape(block_count, Q, groups, CW)
    x_all = blocked[..., :GW].reshape(block_count, Q, groups, HG, P_SIZE)
    b_all = blocked[..., GW : GW + N]
    c_all = blocked[..., GW + N :]
    step_dt = jax.nn.softplus(raw_dt + dt_bias[None]).reshape(block_count, Q, groups, HG)
    decay_rate = -jnp.exp(a_log)
    cumulative = jnp.cumsum(decay_rate[None, None] * step_dt, axis=1)
    causal = lax.broadcasted_iota(jnp.int32, (Q, Q), 0) >= lax.broadcasted_iota(
        jnp.int32, (Q, Q), 1
    )

    def local_block(carried, block_in):
        state_now, factor = carried
        x_blk, b_blk, c_blk, dt_blk, cum_blk = block_in
        scores = jnp.einsum("ign,jgn->gij", c_blk, b_blk, preferred_element_type=jnp.float32)
        cum_cols = jnp.transpose(cum_blk, (1, 2, 0))
        dt_cols = jnp.transpose(dt_blk, (1, 2, 0))
        spread = cum_cols[..., :, None] - cum_cols[..., None, :]
        damping = jnp.where(causal, jnp.exp(jnp.minimum(spread, 0.0)), 0.0)
        weights = (scores[:, None] * damping * dt_cols[..., None, :]).astype(jnp.bfloat16)
        partial_y = jnp.einsum(
            "ghij,jghp->ighp", weights, x_blk, preferred_element_type=jnp.float32
        )
        partial_y = partial_y + d_skip[None, :, :, None] * x_blk
        last_cum = cum_blk[-1]
        tail_factor = jnp.exp(last_cum[None] - cum_blk) * dt_blk
        scaled = (x_blk * tail_factor[..., None]).astype(jnp.bfloat16)
        fresh_state = jnp.einsum(
            "jghp,jgn->ghpn", scaled, b_blk, preferred_element_type=jnp.float32
        )
        keep_blk = jnp.exp(last_cum)
        carried_next = (keep_blk[..., None, None] * state_now + fresh_state, factor * keep_blk)
        return (carried_next, (partial_y, fresh_state, keep_blk))

    zero_state = jnp.zeros((groups, HG, P_SIZE, N), jnp.float32)
    unit_keep = jnp.ones((groups, HG), jnp.float32)
    (local_end, local_keep), (partial_all, fresh_all, keep_all) = lax.scan(
        local_block, (zero_state, unit_keep), (x_all, b_all, c_all, step_dt, cumulative)
    )
    _, incoming = entering((local_keep, local_end), "seq", combine_states, (unit_keep, zero_state))

    def finish_block(state_now, block_in):
        partial_y, fresh_state, keep_blk, c_blk, cum_blk = block_in
        across = jnp.einsum(
            "ign,ghpn->ighp",
            c_blk,
            state_now.astype(jnp.bfloat16),
            preferred_element_type=jnp.float32,
        )
        activity = partial_y + jnp.exp(cum_blk)[..., None] * across
        flat_act = activity.reshape(Q, groups, GW)
        inv_rms = lax.rsqrt(jnp.mean(flat_act * flat_act, axis=-1, keepdims=True) + epsilon)
        normed = (flat_act * inv_rms * norm_gain[None]).astype(jnp.bfloat16)
        return (keep_blk[..., None, None] * state_now + fresh_state, normed)

    _, outputs = lax.scan(
        finish_block, incoming, (partial_all, fresh_all, keep_all, c_all, cumulative)
    )
    return outputs.reshape(row_count, groups * GW)


def per_device(tokens, w_in, conv_w, conv_b, dt_bias, a_log, d_skip, norm_gain):
    gathered = lax.all_gather(tokens, "chan", axis=1, tiled=True)
    return mix_groups(gathered, w_in, conv_w, conv_b, dt_bias, a_log, d_skip, norm_gain)


def solution(mesh):
    return jax.shard_map(
        per_device,
        mesh=mesh,
        in_specs=(
            P("seq", "chan"),
            P("chan", "seq", None),
            P("chan", None, None),
            P("chan", None),
            P("chan", None),
            P("chan", None),
            P("chan", None),
            P("chan", None),
        ),
        out_specs=P("seq", "chan"),
        check_vma=False,
    )
```

profile of v0, /device:TPU:7, one launch (start us, length us, event | category | flops | bytes accessed | tf_op | source)
XLA Modules:
  0.0 446.3 jit_solution(8983873532454136348)
XLA Ops:
  9.8 115.9 %all-gather.7.cloned.1.call-done = bf16[768,4096]{1,0:T(8,128)(2,1)} async-done(((bf16[768,1024]{1,0:T(8,128)(2,1)}), bf16[768,4096]{1,0:T(8,128)(2,1)}) %all-gather.7.cloned.1.call-update) | async-done | bytes 6291472 | tf_op jit(solution)/shard_map/all_gather | solution.py:121
  125.7 112.2 %all-gather.9.cloned.1.call-done = bf16[2,4096,1296]{1,2,0:T(8,128)(2,1)} async-done(((bf16[2,512,1296]{1,2,0:T(8,128)(2,1)}), bf16[2,4096,1296]{1,2,0:T(8,128)(2,1)}) %all-gather.9.cloned.1.call-update) | async-done | bytes 21233680 | tf_op jit(solution)/shard_map/all_gather | solution.py:47
  237.9 22.7 %fusion.48 = (bf16[768,2,1296]{0,2,1:T(8,128)(2,1)}, f32[768,2,1296]{0,2,1:T(8,128)S(1)}) fusion(bf16[2,4096,1296]{1,2,0:T(8,128)(2,1)} %all-gather.9.cloned.1.call-done, bf16[768,4096]{1,0:T(8,128)(2,1)} %all-gather.7.cloned.1.call-done), kind=kOutput, calls=%fused_computation.84 | convolution fusion | flops 16309444608 | bytes 39469056 | tf_op jit(solution)/shard_map/td,gdc->tgc/dot_general | solution.py:44
  261.3 1.4 slice.60
  262.9 1.3 collective-permute-start
  264.5 4.3 slice.61
  269.6 14.2 %multiply_convert_fusion.2 = bf16[768,2,1280]{0,2,1:T(8,128)(2,1)} fusion(bf16[768,2,1280]{0,2,1:T(8,128)(2,1)} %slice.61, bf16[3,2,1280]{0,2,1:T(8,128)(2,1)S(1)} %copy.39, f32[2,1280]{1,0:T(2,128)S(1)} %get-tuple-element.367, f32[2,1280]{1,0:T(2,128)S(1)} %get-tuple-element.368, f32[2,1280]{1,0:T(2,128)S(1)} %get-tuple-element.369, ...), kind=kLoop, calls=%fused_computation.64 | loop fusion | flops 51118080 | bytes 7930880 | tf_op jit(solution)/shard_map/convert_element_type | solution.py:57
  283.9 6.3 %copy.40 = bf16[768,2,1280]{2,0,1:T(8,128)(2,1)} copy(bf16[768,2,1280]{0,2,1:T(8,128)(2,1)} %multiply_convert_fusion.2) | data formatting | bytes 7864320 | tf_op jit(solution)/shard_map/convert_element_type | solution.py:57
  291.4 3.9 slice.66
  295.3 4.7 %copy.41 = bf16[6,128,2,1024]{1,3,2,0:T(8,128)(2,1)} copy(bf16[6,128,2,1024]{3,1,0,2:T(8,128)(2,1)} %slice.66) | data formatting | bytes 6291456 | tf_op jit(solution)/shard_map/slice | solution.py:60
  300.0 37.4 %while.45 = (s32[]{:T(128)}, f32[2,16,64,128]{3,2,1,0:T(8,128)S(1)}, f32[2,16]{1,0:T(2,128)S(1)}, f32[6,128,2,16,64]{1,4,3,2,0:T(8,128)}, f32[6,2,16,64,128]{4,3...) while((s32[]{:T(128)}, ...), condition=%wide.region_2.3_spmd.clone, body=%wide.region_1.2_spmd.clone.sunk | while | flops 148136000 | bytes 8544967 | solution.py:95
  300.5 1.5 fusion.67
  302.0 3.2 fusion.69
  306.7 1.5 fusion.67
  308.2 3.2 fusion.69
  313.0 1.5 fusion.67
  314.4 3.1 fusion.69
  319.2 1.5 fusion.67
  320.6 3.2 fusion.69
  325.4 1.5 fusion.67
  326.9 3.2 fusion.69
  331.7 1.5 fusion.67
  333.2 3.2 fusion.69
  338.4 9.8 %all-gather.2 = f32[8,2,16]{2,1,0:T(2,128)S(1)} all-gather(f32[1,2,16]{2,1,0:T(2,128)S(1)} %bitcast.159), channel_id=2, replica_groups=mesh['seq'=8,'chan'=4] {'seq'}, dimensions={0}, use_global_device_ids=true | all-gather | bytes 1152 | tf_op jit(solution)/shard_map/all_gather | solution.py:26
  348.2 45.7 %all-gather.11.cloned.1.call-done = f32[16,16,64,128]{3,2,1,0:T(8,128)} async-done(((f32[2,16,64,128]{3,2,1,0:T(8,128)}), f32[16,16,64,128]{3,2,1,0:T(8,128)}) %all-gather.11.cloned.1.call-update) | async-done | bytes 8388624 | tf_op jit(solution)/shard_map/all_gather | solution.py:26
  394.0 10.6 %while.43 = (s32[]{:T(128)}, f32[2,16,64,128]{3,2,1,0:T(8,128)S(1)}, s32[]{:T(128)}, f32[8,2,16]{2,1,0:T(2,128)S(1)}, f32[8,2,16,64,128]{4,3,2,1,0:T(8,128)}, /*index=5*/s32[]{:T(128)}, s32[]{:T(128)}, s32[]{:T(128)}) while((s32[]{:T(128)}, f32[2,16,64,128]{3,2,1,0:T(8,128)S(1)}, s32[]{:T(128)}, f32[8,2,16]{2,1,0:T(2,128)S(1)}, ...), condition=%wide.region_4.5_spmd, body=%wide.region_3.4_spmd.sunk | while | flops 524293 | bytes 3146247 | solution.py:34
  394.1 1.4 bitcast_add_fusion.4
  395.6 1.4 bitcast_add_fusion.4
  397.0 1.4 bitcast_add_fusion.4
  398.5 1.4 bitcast_add_fusion.4
  400.0 1.4 bitcast_add_fusion.4
  401.5 1.4 bitcast_add_fusion.4
  403.0 1.4 bitcast_add_fusion.4
  404.7 30.5 %while.44 = (s32[]{:T(128)}, f32[2,16,64,128]{3,2,1,0:T(8,128)S(1)}, bf16[6,128,2,1024]{3,2,1,0:T(2,128)(2,1)}, f32[6,2,16]{2,1,0:T(2,128)S(1)}, f32[6,2,16,64,1...) while((s32[]{:T(128)}, ...), condition=%wide.region_7.8_spmd, body=%wide.region_5.7_spmd.sunk | while | flops 69730560 | bytes 10089981 | solution.py:114
  404.7 1.6 multiply_reduce_fusion.2
  407.1 1.4 bitcast_add_fusion.5
  408.6 1.2 constant_dynamic-update-slice_fusion.4
  409.8 1.5 multiply_reduce_fusion.2
  412.2 1.4 bitcast_add_fusion.5
  414.9 1.5 multiply_reduce_fusion.2
  417.3 1.4 bitcast_add_fusion.5
  420.0 1.6 multiply_reduce_fusion.2
  422.4 1.4 bitcast_add_fusion.5
  425.0 1.6 multiply_reduce_fusion.2
  427.5 1.4 bitcast_add_fusion.5
  430.1 1.6 multiply_reduce_fusion.2
  432.5 1.4 bitcast_add_fusion.5
  435.1 4.6 %copy.59 = bf16[96,8,2,1024]{3,1,2,0:T(8,128)(2,1)} copy(bf16[96,8,2,1024]{3,2,1,0:T(2,128)(2,1)} %bitcast.156) | data formatting | bytes 6291456
  (134 shorter events, 27.9 us)
Async XLA Ops:
  6.5 119.2 %all-gather.7.cloned.1.call-start = ((), (), s32[]{:S(2)}) async-start(), calls=%async_computation | async-start | bytes 7864320 | tf_op jit(solution)/shard_map/all_gather | solution.py:121
  7.3 230.7 %all-gather.9.cloned.1.call-start = ((), (), s32[]{:S(2)}) async-start(), calls=%async_computation.1 | async-start | bytes 23887872 | tf_op jit(solution)/shard_map/all_gather | solution.py:47
  8.0 385.9 %all-gather.11.cloned.1.call-start = ((), (), s32[]{:S(2)}) async-start(), calls=%async_computation.2 | async-start | bytes 9437184 | tf_op jit(solution)/shard_map/all_gather | solution.py:26
  9.8 250.8 %copy-start.3 = (f32[2,16]{1,0:T(2,128)S(1)}, f32[2,16]{1,0:T(2,128)}, u32[]{:S(2)}) copy-start(f32[2,16]{1,0:T(2,128)} %param.18) | copy-start | bytes 388
  261.3 8.4 %copy-start.2 = (f32[2,1280]{1,0:T(2,128)S(1)}, f32[2,1280]{1,0:T(2,128)}, u32[]{:S(2)}) copy-start(f32[2,1280]{1,0:T(2,128)} %param.17) | copy-start | bytes 30724
  262.9 6.3 %collective-permute-start = (bf16[3,2,1280]{2,1,0:T(2,128)(2,1)S(1)}, bf16[3,2,1280]{2,1,0:T(2,128)(2,1)S(1)}, u32[]{:S(2)}, u32[]{:S(2)}) collective-permute-start(bf16[3,2,1280]{2,1,0:T(2,128)(2,1)S(1)} %copy.38), channel_id=1, source_target_pairs={{0,4},{4,8},{8,12},{12,16},{16,20},{20,24},{24,28},{1,5},{5,9},{9,... | collective-permute-start | bytes 46088 | tf_op jit(solution)/shard_map/ppermute | solution.py:21
  291.4 8.6 %copy-start.4 = (f32[2,16]{1,0:T(2,128)S(1)}, f32[2,16]{1,0:T(2,128)}, u32[]{:S(2)}) copy-start(f32[2,16]{1,0:T(2,128)} %param.20) | copy-start | bytes 388
  337.4 1.0 copy-start
  394.0 10.6 %copy-start.1 = (f32[2,1024]{1,0:T(2,128)S(1)}, f32[2,1024]{1,0:T(2,128)}, u32[]{:S(2)}) copy-start(f32[2,1024]{1,0:T(2,128)} %param.21) | copy-start | bytes 24580
Sparse Core Ops, SparseCore 0:
  8.9 116.7 all-gather.6
  127.6 110.3 all-gather.8
  338.5 55.3 all-gather.10
where the time goes:
time: 448 us; the launch traced here: 446 us
  waiting for transfers between devices  275 us (61%)
  matrix products  60.9 us (14%)
  local copies, waits for them, and re-layouts  47.7 us (11%)
  other arithmetic  37 us (8%)
  between operations  13.3 us (3%)
  blocking collectives  9.81 us (2%)
    all_gather x1, waiting for transfers between devices, per_device(): gathered = lax.all_gather(tokens, 'chan', axis=1, tiled=True)  116 us
    all_gather x1, waiting for transfers between devices, mix_groups(): lax.all_gather(w_in, 'seq', axis=1, tiled=True)  112 us
    all_gather x1, waiting for transfers between devices, entering(): gathered = jax.tree.map(lambda a: lax.all_gather(a, axis), part)  45.7 us
    dot_general x1, matrix products, mix_groups(): jnp.einsum('td,gdc->tgc', gathered, lax.all_gather(w_in, 'seq', axis=1, t...  22.7 us
    dot_general x6, matrix products, local_block(): jnp.einsum('ghij,jghp->ighp', weights, x_blk, preferred_element_type=jnp....  19 us
    convert_element_type x1, other arithmetic, mix_groups(): inputs = jax.nn.silu(pre_act).astype(jnp.bfloat16)  14.2 us
    dynamic_update_slice x12, local copies, waits for them, and re-layouts, mix_groups(): lax.scan(finish_block, incoming, (partial_all, fresh_all, keep_all, c_all...  10.1 us
    add x7, other arithmetic, combine_states(): later_one[0][..., None, None] * earlier[1] + later_one[1]  10.1 us
  transfers between devices with their start and end apart: 4, of which 3 were waited for; matrix products, arithmetic and copies ran while one was open for 1% of the time, Pallas kernels for 0%

commit v1 on v0

--- a/solution.py
+++ b/solution.py
@@ -1,6 +1,9 @@
+import functools
 import jax
 import jax.numpy as jnp
 from jax import lax
+from jax.experimental import pallas as pl
+from jax.experimental.pallas import tpu as pltpu
 from jax.sharding import PartitionSpec as P
 
 P_SIZE = 64
@@ -10,9 +13,223 @@
 HG = 16
 GW = 1024
 CW = 1280
-
+RIM = 16
+MESH = pl.DeviceIdType.MESH
 
 epsilon = 1e-05
+
+
+def project_kernel(
+    lines, tok_ref, w_ref, conv_ref, dt_ref, rim_ref,
+    tok_all, w_all, acc, own_sem, tok_send, tok_recv, w_own, w_fwd, w_sib, w_recv,
+):
+    s = lax.axis_index("seq")
+    c = lax.axis_index("chan")
+    groups, cols, depth = w_ref.shape
+    rows, feats = tok_ref.shape
+    half = rows // 2
+    ratio = feats // depth
+    core = s % 2
+    sib = s + 1 - 2 * core
+    xs = s + 2 - 4 * ((s // 2) % 2)
+    ys = s + 4 - 8 * ((s // 4) % 2)
+    diag = xs + ys - s
+    fwd_shard = xs * (1 - core) + ys * core
+    fwd_to = ys * (1 - core) + xs * core
+
+    barrier = pltpu.get_barrier_semaphore()
+    for other in (sib, xs, ys):
+        pl.semaphore_signal(barrier, inc=1, device_id={"seq": other}, device_id_type=MESH)
+
+    @pl.when(c > 0)
+    def _():
+        pl.semaphore_signal(barrier, inc=1, device_id={"chan": c - 1}, device_id_type=MESH)
+
+    @pl.when(c < lines - 1)
+    def _():
+        pl.semaphore_signal(barrier, inc=1, device_id={"chan": c + 1}, device_id_type=MESH)
+
+    pl.semaphore_wait(barrier, 3 + jnp.minimum(c, 1) + jnp.minimum(lines - 1 - c, 1))
+
+    def tok_copy(shard, part, way, own):
+        window = pl.ds(part * half, half)
+        src = tok_ref.at[window] if own else tok_all.at[shard, window]
+        return pltpu.make_async_remote_copy(
+            src_ref=src,
+            dst_ref=tok_all.at[shard, window],
+            send_sem=tok_send.at[way, shard, part],
+            recv_sem=tok_recv.at[shard, part],
+            device_id={"chan": c + (1 if way else -1)},
+            device_id_type=MESH,
+        )
+
+    def w_copy(shard, g, sem, to, own):
+        src = w_ref.at[g] if own else w_all.at[shard, g]
+        return pltpu.make_async_remote_copy(
+            src_ref=src,
+            dst_ref=w_all.at[shard, g],
+            send_sem=sem,
+            recv_sem=w_recv.at[shard, g],
+            device_id={"seq": to},
+            device_id_type=MESH,
+        )
+
+    def tok_sends(k, part, act):
+        @pl.when((c - k >= 0) & (c < lines - 1))
+        def _():
+            act(tok_copy(c - k, part, 1, k == 0))
+
+        @pl.when((c + k < lines) & (c > 0))
+        def _():
+            act(tok_copy(c + k, part, 0, k == 0))
+
+    def tok_arrive(k, part):
+        @pl.when(c - k >= 0)
+        def _():
+            tok_copy(c - k, part, 1, False).wait_recv()
+
+        @pl.when(c + k < lines)
+        def _():
+            tok_copy(c + k, part, 0, False).wait_recv()
+
+    def start(copy):
+        copy.start()
+
+    def sent(copy):
+        copy.wait_send()
+
+    own_tok = pltpu.make_async_copy(tok_ref, tok_all.at[c], own_sem.at[0])
+    own_w = pltpu.make_async_copy(w_ref, w_all.at[s], own_sem.at[1])
+    for part in range(2):
+        tok_sends(0, part, start)
+        for i, to in enumerate((xs, ys, sib)):
+            w_copy(s, part, w_own.at[i, part], to, True).start()
+    own_tok.start()
+    own_w.start()
+
+    def near_weights(g):
+        w_copy(xs, g, w_sib.at[0, g], sib, False).wait_recv()
+        w_copy(ys, g, w_sib.at[1, g], sib, False).wait_recv()
+        w_copy(fwd_shard, g, w_fwd.at[g], fwd_to, False).start()
+        w_copy(xs, g, w_sib.at[0, g], sib, False).start()
+        w_copy(ys, g, w_sib.at[1, g], sib, False).start()
+
+    def far_weights(g):
+        w_copy(diag, g, w_sib.at[2, g], sib, False).wait_recv()
+        w_copy(diag, g, w_sib.at[2, g], sib, False).start()
+
+    def relay(k, part):
+        tok_arrive(k, part)
+        if k < lines - 1:
+            tok_sends(k, part, start)
+
+    relay(1, 0)
+    near_weights(0)
+    relay(1, 1)
+    if lines > 2:
+        relay(2, 0)
+    near_weights(1)
+    if lines > 2:
+        relay(2, 1)
+    far_weights(0)
+    far_weights(1)
+    for k in range(3, lines - 1):
+        relay(k, 0)
+        relay(k, 1)
+    for shard in (sib, sib + xs - s, sib + ys - s, sib + diag - s):
+        for g in range(groups):
+            w_copy(shard, g, w_own.at[2, g], sib, False).wait_recv()
+    own_tok.wait()
+    own_w.wait()
+
+    tiles = 3
+    tall = cols // tiles
+
+    def product(shard, first):
+        @pl.loop(0, groups * tiles)
+        def _(step):
+            g = step // tiles
+            window = pl.ds(pl.multiple_of((step % tiles) * tall, 16), tall)
+            total = None
+            for i in range(ratio):
+                term = lax.dot_general(
+                    w_all[shard * ratio + i, g, window, :],
+                    tok_all[shard, :, i * depth : (i + 1) * depth],
+                    (((1,), (1,)), ((), ())),
+                    preferred_element_type=jnp.float32,
+                )
+                total = term if total is None else total + term
+            if first:
+                acc[g, window, :] = total
+            else:
+                acc[g, window, :] += total
+
+    product(c, True)
+    for k in range(1, lines):
+        if k >= 3 and k == lines - 1:
+            tok_arrive(k, 0)
+            tok_arrive(k, 1)
+
+        @pl.when(c - k >= 0)
+        def _():
+            product(c - k, False)
+
+        @pl.when(c + k < lines)
+        def _():
+            product(c + k, False)
+
+    for g in range(groups):
+        conv_ref[g] = acc[g, :CW, :].astype(jnp.bfloat16)
+        dt_ref[g] = acc[g, CW:, :]
+        rim_ref[g] = acc[g, :CW, rows - Q :].T[Q - RIM :].astype(jnp.bfloat16)
+
+    for part in range(2):
+        for k in range(lines - 1):
+            tok_sends(k, part, sent)
+        for i, to in enumerate((xs, ys, sib)):
+            w_copy(s, part, w_own.at[i, part], to, True).wait_send()
+        w_copy(fwd_shard, part, w_fwd.at[part], fwd_to, False).wait_send()
+        w_copy(xs, part, w_sib.at[0, part], sib, False).wait_send()
+        w_copy(ys, part, w_sib.at[1, part], sib, False).wait_send()
+        w_copy(diag, part, w_sib.at[2, part], sib, False).wait_send()
+
+
+def project(tokens, w_turned, lines, ranks):
+    groups, cols, depth = w_turned.shape
+    rows, feats = tokens.shape
+    shapes = (
+        jax.ShapeDtypeStruct((groups, CW, rows), jnp.bfloat16),
+        jax.ShapeDtypeStruct((groups, cols - CW, rows), jnp.float32),
+        jax.ShapeDtypeStruct((groups, RIM, CW), jnp.bfloat16),
+    )
+    if ranks == 8 and groups == 2 and lines > 1:
+        dma = pltpu.SemaphoreType.DMA
+        return pl.pallas_call(
+            functools.partial(project_kernel, lines),
+            out_shape=shapes,
+            in_specs=[pl.BlockSpec(memory_space=pl.ANY)] * 2,
+            out_specs=(pl.BlockSpec(memory_space=pltpu.VMEM),) * 3,
+            scratch_shapes=[
+                pltpu.VMEM((lines, rows, feats), jnp.bfloat16),
+                pltpu.VMEM((ranks, groups, cols, depth), jnp.bfloat16),
+                pltpu.VMEM((groups, cols, rows), jnp.float32),
+                dma((2,)),
+                dma((2, lines, 2)),
+                dma((lines, 2)),
+                dma((3, 2)),
+                dma((2,)),
+                dma((3, 2)),
+                dma((ranks, 2)),
+            ],
+            compiler_params=pltpu.CompilerParams(
+                collective_id=0, has_side_effects=True, vmem_limit_bytes=56 * 2**20
+            ),
+        )(tokens, w_turned)
+    gathered = lax.all_gather(tokens, "chan", axis=1, tiled=True)
+    whole = lax.all_gather(w_turned, "seq", axis=2, tiled=True)
+    turned = jnp.einsum("gcd,td->gct", whole, gathered, preferred_element_type=jnp.float32)
+    conv = turned[:, :CW].astype(jnp.bfloat16)
+    return conv, turned[:, CW:], jnp.swapaxes(conv[:, :, rows - RIM :], 1, 2)
 
 
 def shifted(block, axis, distance):
@@ -38,18 +255,15 @@
     return (earlier[0] * later_one[0], later_one[0][..., None, None] * earlier[1] + later_one[1])
 
 
-def mix_groups(gathered, w_in, conv_w, conv_b, dt_bias, a_log, d_skip, norm_gain):
+def mix_groups(tokens, w_in, conv_w, conv_b, dt_bias, a_log, d_skip, norm_gain):
     groups = w_in.shape[0]
-    row_count = gathered.shape[0]
-    projected = jnp.einsum(
-        "td,gdc->tgc",
-        gathered,
-        lax.all_gather(w_in, "seq", axis=1, tiled=True),
-        preferred_element_type=jnp.float32,
-    )
-    conv_in = projected[:, :, :CW].astype(jnp.bfloat16)
-    raw_dt = projected[gathered.shape[0] - row_count :, :, CW:]
-    rim_rows = shifted(conv_in[row_count - (KCONV - 1) :], "seq", 1)
+    row_count = tokens.shape[0]
+    conv_turned, dt_turned, rim = project(
+        tokens, jnp.swapaxes(w_in, 1, 2), lax.axis_size("chan"), lax.axis_size("seq")
+    )
+    conv_in = jnp.transpose(conv_turned, (2, 0, 1))
+    raw_dt = jnp.transpose(dt_turned, (2, 0, 1))
+    rim_rows = jnp.swapaxes(shifted(rim, "seq", 1)[:, RIM - (KCONV - 1) :], 0, 1)
     padded = jnp.concatenate([rim_rows, conv_in], axis=0)
     pre_act = jnp.broadcast_to(conv_b[None], (row_count, groups, CW))
     for offset in range(KCONV):
@@ -118,8 +332,7 @@
 
 
 def per_device(tokens, w_in, conv_w, conv_b, dt_bias, a_log, d_skip, norm_gain):
-    gathered = lax.all_gather(tokens, "chan", axis=1, tiled=True)
-    return mix_groups(gathered, w_in, conv_w, conv_b, dt_bias, a_log, d_skip, norm_gain)
+    return mix_groups(tokens, w_in, conv_w, conv_b, dt_bias, a_log, d_skip, norm_gain)
 
 
 def solution(mesh):

time: 448 us -> 307 us (0.69)
  waiting for transfers between devices: 275 us -> 45.5 us
  Pallas kernels: 0 us -> 116 us
  matrix products: 60.9 us -> 38.1 us
  local copies, waits for them, and re-layouts: 47.7 us -> 41.5 us
    all_gather x2 -> x0, waiting for transfers between devices: 228 us -> none  [the longest x1 116 us: per_device(): gathered = lax.all_gather(tokens, 'chan', axis=1, tiled=True)]
    pallas_call x0 -> x1, Pallas kernels: none -> 116 us  [project(): pl.pallas_call(functools.partial(project_kernel, lines), out_shape=shapes...]
    dot_general x1 -> x0, matrix products: 22.7 us -> none  [mix_groups(): jnp.einsum('td,gdc->tgc', gathered, lax.all_gather(w_in, 'seq', axis=1, t...]
    slice x3 -> x0, local copies, waits for them, and re-layouts: 5.98 us -> none  [the longest x1 4.35 us: mix_groups(): conv_in = projected[:, :, :CW].astype(jnp.bfloat16)]
  transfers between devices with their start and end apart: 4 -> 2, of which waited for: 3 -> 1; matrix products, arithmetic and copies ran while one was open for 1% -> 1% of each run, Pallas kernels for 0% -> 0%
where the time goes in v1:
time: 307 us; the launch traced here: 305 us
  Pallas kernels  116 us (38%)
  waiting for transfers between devices  45.5 us (15%)
  local copies, waits for them, and re-layouts  41.5 us (14%)
  matrix products  38.1 us (12%)
  other arithmetic  37.8 us (12%)
  between operations  13.6 us (4%)
  blocking collectives  10.4 us (3%)
    pallas_call x1, Pallas kernels, project(): pl.pallas_call(functools.partial(project_kernel, lines), out_shape=shapes...  116 us
    all_gather x1, waiting for transfers between devices, entering(): gathered = jax.tree.map(lambda a: lax.all_gather(a, axis), part)  45.5 us
    dot_general x6, matrix products, local_block(): jnp.einsum('ghij,jghp->ighp', weights, x_blk, preferred_element_type=jnp....  19 us
    convert_element_type x1, other arithmetic, mix_groups(): inputs = jax.nn.silu(pre_act).astype(jnp.bfloat16)  14.2 us
    all_gather x1, blocking collectives, entering(): gathered = jax.tree.map(lambda a: lax.all_gather(a, axis), part)  10.4 us
    add x7, other arithmetic, combine_states(): later_one[0][..., None, None] * earlier[1] + later_one[1]  10.1 us
    dynamic_update_slice x12, local copies, waits for them, and re-layouts, mix_groups(): lax.scan(finish_block, incoming, (partial_all, fresh_all, keep_all, c_all...  10.1 us
    dot_general x6, matrix products, finish_block(): jnp.einsum('ign,ghpn->ighp', c_blk, state_now.astype(jnp.bfloat16), prefe...  9.3 us
  transfers between devices with their start and end apart: 2, of which 1 were waited for; matrix products, arithmetic and copies ran while one was open for 1% of the time, Pallas kernels for 0%

profile of v1, /device:TPU:7, one launch (start us, length us, event | category | flops | bytes accessed | tf_op | source)
XLA Modules:
  0.0 304.8 jit_solution(3513107844964149428)
XLA Ops:
  6.5 115.7 %shard_map.82 = (bf16[2,1280,768]{2,1,0:T(8,128)(2,1)}, f32[2,16,768]{2,1,0:T(8,128)}, bf16[2,16,1280]{2,1,0:T(8,128)(2,1)}) custom-call(bf16[768,1024]{1,0:T(8,128)(2,1)} %tok_ref.1, bf16[2,1296,512]{2,1,0:T(8,128)(2,1)} %bitcast.172), custom_call_target="tpu_custom_call" | custom-call | tf_op jit(solution)/shard_map/pallas_call | solution.py:207
  122.2 1.3 collective-permute-start
  127.9 14.2 %multiply_convert_fusion.2 = bf16[768,2,1280]{0,2,1:T(8,128)(2,1)} fusion(bf16[768,2,1280]{0,2,1:T(8,128)(2,1)} %bitcast.169, bf16[3,2,1280]{0,2,1:T(8,128)(2,1)S(1)} %copy.41, f32[2,1280]{1,0:T(2,128)S(1)} %get-tuple-element.371, f32[2,1280]{1,0:T(2,128)S(1)} %get-tuple-element.372, f32[2,1280]{1,0:T(2,128)S(1)} %get-tuple-element.373, ...), kind=kLoop, calls=%fused_computation.64 | loop fusion | flops 51118080 | bytes 7930880 | tf_op jit(solution)/shard_map/convert_element_type | solution.py:271
  142.0 6.1 %copy.42 = bf16[768,2,1280]{2,0,1:T(8,128)(2,1)} copy(bf16[768,2,1280]{0,2,1:T(8,128)(2,1)} %multiply_convert_fusion.2) | data formatting | bytes 7864320 | tf_op jit(solution)/shard_map/convert_element_type | solution.py:271
  148.1 1.2 fusion.48
  149.3 3.9 %slice.54 = bf16[6,128,2,1024]{3,1,0,2:T(8,128)(2,1)} slice(bf16[6,128,2,1280]{3,1,0,2:T(8,128)(2,1)} %bitcast.167), slice={[0:6], [0:128], [0:2], [0:1024]} | slice | bytes 6291456 | tf_op jit(solution)/shard_map/slice | solution.py:274
  153.2 4.7 %copy.43 = bf16[6,128,2,1024]{1,3,2,0:T(8,128)(2,1)} copy(bf16[6,128,2,1024]{3,1,0,2:T(8,128)(2,1)} %slice.54) | data formatting | bytes 6291456 | tf_op jit(solution)/shard_map/slice | solution.py:274
  157.9 37.3 %while.45 = (s32[]{:T(128)}, f32[2,16,64,128]{3,2,1,0:T(8,128)S(1)}, f32[2,16]{1,0:T(2,128)S(1)}, f32[6,128,2,16,64]{1,4,3,2,0:T(8,128)}, f32[6,2,16,64,128]{4,3...) while((s32[]{:T(128)}, ...), condition=%wide.region_2.3_spmd.clone, body=%wide.region_1.2_spmd.clone.sunk | while | flops 148136000 | bytes 8544956 | solution.py:309
  158.2 1.5 fusion.67
  160.9 3.2 %fusion.69 = f32[6,128,2,16,64]{1,4,3,2,0:T(8,128)} fusion(f32[6,128,2,16,64]{1,4,3,2,0:T(8,128)} %get-tuple-element.569, s32[]{:T(128)} %get-tuple-element.566, f32[2,16,128]{2,1,0:T(8,128)S(1)} %bitcast.174, f32[2,16,128]{2,1,0:T(8,128)S(1)} %dynamic-slice_bitcast_fusion.5, f32[2,128,128]{2,1,0:T(8,128)S(1)} %fusion.68, ...), kind=kOutput, calls=%fused_computation.24.clone.1 | convolution fusion | flops 71041024 | bytes 2295808 | tf_op jit(solution)/shard_map/while/body/eval_jaxpr/ghij,jghp->ighp/dot_general | solution.py:293
  164.5 1.5 fusion.67
  167.2 3.1 %fusion.69 = f32[6,128,2,16,64]{1,4,3,2,0:T(8,128)} fusion(f32[6,128,2,16,64]{1,4,3,2,0:T(8,128)} %get-tuple-element.569, s32[]{:T(128)} %get-tuple-element.566, f32[2,16,128]{2,1,0:T(8,128)S(1)} %bitcast.174, f32[2,16,128]{2,1,0:T(8,128)S(1)} %dynamic-slice_bitcast_fusion.5, f32[2,128,128]{2,1,0:T(8,128)S(1)} %fusion.68, ...), kind=kOutput, calls=%fused_computation.24.clone.1 | convolution fusion | flops 71041024 | bytes 2295808 | tf_op jit(solution)/shard_map/while/body/eval_jaxpr/ghij,jghp->ighp/dot_general | solution.py:293
  170.6 1.5 fusion.67
  173.3 3.1 %fusion.69 = f32[6,128,2,16,64]{1,4,3,2,0:T(8,128)} fusion(f32[6,128,2,16,64]{1,4,3,2,0:T(8,128)} %get-tuple-element.569, s32[]{:T(128)} %get-tuple-element.566, f32[2,16,128]{2,1,0:T(8,128)S(1)} %bitcast.174, f32[2,16,128]{2,1,0:T(8,128)S(1)} %dynamic-slice_bitcast_fusion.5, f32[2,128,128]{2,1,0:T(8,128)S(1)} %fusion.68, ...), kind=kOutput, calls=%fused_computation.24.clone.1 | convolution fusion | flops 71041024 | bytes 2295808 | tf_op jit(solution)/shard_map/while/body/eval_jaxpr/ghij,jghp->ighp/dot_general | solution.py:293
  176.8 1.5 fusion.67
  179.5 3.2 %fusion.69 = f32[6,128,2,16,64]{1,4,3,2,0:T(8,128)} fusion(f32[6,128,2,16,64]{1,4,3,2,0:T(8,128)} %get-tuple-element.569, s32[]{:T(128)} %get-tuple-element.566, f32[2,16,128]{2,1,0:T(8,128)S(1)} %bitcast.174, f32[2,16,128]{2,1,0:T(8,128)S(1)} %dynamic-slice_bitcast_fusion.5, f32[2,128,128]{2,1,0:T(8,128)S(1)} %fusion.68, ...), kind=kOutput, calls=%fused_computation.24.clone.1 | convolution fusion | flops 71041024 | bytes 2295808 | tf_op jit(solution)/shard_map/while/body/eval_jaxpr/ghij,jghp->ighp/dot_general | solution.py:293
  183.0 1.5 fusion.67
  185.8 3.2 %fusion.69 = f32[6,128,2,16,64]{1,4,3,2,0:T(8,128)} fusion(f32[6,128,2,16,64]{1,4,3,2,0:T(8,128)} %get-tuple-element.569, s32[]{:T(128)} %get-tuple-element.566, f32[2,16,128]{2,1,0:T(8,128)S(1)} %bitcast.174, f32[2,16,128]{2,1,0:T(8,128)S(1)} %dynamic-slice_bitcast_fusion.5, f32[2,128,128]{2,1,0:T(8,128)S(1)} %fusion.68, ...), kind=kOutput, calls=%fused_computation.24.clone.1 | convolution fusion | flops 71041024 | bytes 2295808 | tf_op jit(solution)/shard_map/while/body/eval_jaxpr/ghij,jghp->ighp/dot_general | solution.py:293
  189.2 1.5 fusion.67
  192.0 3.2 %fusion.69 = f32[6,128,2,16,64]{1,4,3,2,0:T(8,128)} fusion(f32[6,128,2,16,64]{1,4,3,2,0:T(8,128)} %get-tuple-element.569, s32[]{:T(128)} %get-tuple-element.566, f32[2,16,128]{2,1,0:T(8,128)S(1)} %bitcast.174, f32[2,16,128]{2,1,0:T(8,128)S(1)} %dynamic-slice_bitcast_fusion.5, f32[2,128,128]{2,1,0:T(8,128)S(1)} %fusion.68, ...), kind=kOutput, calls=%fused_computation.24.clone.1 | convolution fusion | flops 71041024 | bytes 2295808 | tf_op jit(solution)/shard_map/while/body/eval_jaxpr/ghij,jghp->ighp/dot_general | solution.py:293
  196.2 10.4 %all-gather.2 = f32[8,2,16]{2,1,0:T(2,128)S(1)} all-gather(f32[1,2,16]{2,1,0:T(2,128)S(1)} %bitcast.175), channel_id=2, replica_groups=mesh['seq'=8,'chan'=4] {'seq'}, dimensions={0}, use_global_device_ids=true | all-gather | bytes 1152 | tf_op jit(solution)/shard_map/all_gather | solution.py:243
  206.6 45.5 %all-gather.5.cloned.1.call-done = f32[16,16,64,128]{3,2,1,0:T(8,128)} async-done(((f32[2,16,64,128]{3,2,1,0:T(8,128)}), f32[16,16,64,128]{3,2,1,0:T(8,128)}) %all-gather.5.cloned.1.call-update) | async-done | bytes 8388624 | tf_op jit(solution)/shard_map/all_gather | solution.py:243
  252.2 10.6 %while.43 = (s32[]{:T(128)}, f32[2,16,64,128]{3,2,1,0:T(8,128)S(1)}, s32[]{:T(128)}, f32[8,2,16]{2,1,0:T(2,128)S(1)}, f32[8,2,16,64,128]{4,3,2,1,0:T(8,128)}, /*index=5*/s32[]{:T(128)}, s32[]{:T(128)}, s32[]{:T(128)}) while((s32[]{:T(128)}, f32[2,16,64,128]{3,2,1,0:T(8,128)S(1)}, s32[]{:T(128)}, f32[8,2,16]{2,1,0:T(2,128)S(1)}, ...), condition=%wide.region_4.5_spmd, body=%wide.region_3.4_spmd.sunk | while | flops 524293 | bytes 3146239 | solution.py:251
  252.4 1.4 bitcast_add_fusion.4
  253.9 1.4 bitcast_add_fusion.4
  255.4 1.4 bitcast_add_fusion.4
  256.9 1.4 bitcast_add_fusion.4
  258.4 1.4 bitcast_add_fusion.4
  259.9 1.4 bitcast_add_fusion.4
  261.4 1.4 bitcast_add_fusion.4
  262.9 30.5 %while.44 = (s32[]{:T(128)}, f32[2,16,64,128]{3,2,1,0:T(8,128)S(1)}, bf16[6,128,2,1024]{3,2,1,0:T(2,128)(2,1)}, f32[6,2,16]{2,1,0:T(2,128)S(1)}, f32[6,2,16,64,1...) while((s32[]{:T(128)}, ...), condition=%wide.region_7.8_spmd, body=%wide.region_5.7_spmd.sunk | while | flops 69730560 | bytes 10090481 | solution.py:328
  262.9 1.6 multiply_reduce_fusion.2
  265.3 1.2 constant_dynamic-update-slice_fusion.4
  266.5 1.4 bitcast_add_fusion.5
  268.0 1.5 multiply_reduce_fusion.2
  271.6 1.4 bitcast_add_fusion.5
  273.1 1.6 multiply_reduce_fusion.2
  275.5 1.2 constant_dynamic-update-slice_fusion.4
  276.7 1.4 bitcast_add_fusion.5
  278.2 1.5 multiply_reduce_fusion.2
  281.8 1.4 bitcast_add_fusion.5
  283.3 1.5 multiply_reduce_fusion.2
  285.7 1.2 constant_dynamic-update-slice_fusion.4
  286.9 1.4 bitcast_add_fusion.5
  288.3 1.6 multiply_reduce_fusion.2
  290.8 1.2 constant_dynamic-update-slice_fusion.4
  292.0 1.4 bitcast_add_fusion.5
  293.4 4.6 %copy.61 = bf16[96,8,2,1024]{3,1,2,0:T(8,128)(2,1)} copy(bf16[96,8,2,1024]{3,2,1,0:T(2,128)(2,1)} %bitcast.171) | data formatting | bytes 6291456
  (124 shorter events, 22.2 us)
Async XLA Ops:
  6.5 121.3 %copy-start.2 = (f32[2,1280]{1,0:T(2,128)S(1)}, f32[2,1280]{1,0:T(2,128)}, u32[]{:S(2)}) copy-start(f32[2,1280]{1,0:T(2,128)} %param.17) | copy-start | bytes 30724
  6.5 245.5 %all-gather.5.cloned.1.call-start = ((), (), s32[]{:S(2)}) async-start(), calls=%async_computation | async-start | bytes 9437184 | tf_op jit(solution)/shard_map/all_gather | solution.py:243
  122.2 5.2 %collective-permute-start = (bf16[2,16,1280]{2,1,0:T(8,128)(2,1)}, bf16[2,16,1280]{2,1,0:T(8,128)(2,1)S(1)}, u32[]{:S(2)}, u32[]{:S(2)}) collective-permute-start(bf16[2,16,1280]{2,1,0:T(8,128)(2,1)} %get-tuple-element.171), channel_id=1, source_target_pairs={{0,4},{4,8},{8,12},{12,16},{16,20},{20,24},{24,28},{1,5},{5,9},{9,... | collective-permute-start | bytes 245768 | tf_op jit(solution)/shard_map/ppermute | solution.py:238
  149.3 8.6 %copy-start.3 = (f32[2,16]{1,0:T(2,128)S(1)}, f32[2,16]{1,0:T(2,128)}, u32[]{:S(2)}) copy-start(f32[2,16]{1,0:T(2,128)} %param.20) | copy-start | bytes 388
  195.2 1.0 copy-start
  252.2 10.7 %copy-start.1 = (f32[2,1024]{1,0:T(2,128)S(1)}, f32[2,1024]{1,0:T(2,128)}, u32[]{:S(2)}) copy-start(f32[2,1024]{1,0:T(2,128)} %param.21) | copy-start | bytes 24580
Sparse Core Ops, SparseCore 0:
  196.3 55.7 all-gather.4

commit v2 on v1

--- a/solution.py
+++ b/solution.py
@@ -232,107 +232,255 @@
     return conv, turned[:, CW:], jnp.swapaxes(conv[:, :, rows - RIM :], 1, 2)
 
 
+def mix_kernel(
+    ranks, conv_ref, dt_ref, rim_ref, par_ref, head_ref, skip_ref,
+    part_ref, c_ref, dec_ref, in_ref,
+    act, rim_t, dts, cums, states, total, keep, before, keep_before,
+    out_state, out_keep, got_state, got_keep, send_sem, recv_sem,
+):
+    s = lax.axis_index("seq")
+    groups, _, rows = conv_ref.shape
+    blocks = rows // Q
+    steps = ranks.bit_length() - 1
+    partners = [s + 2**i - 2 ** (i + 1) * ((s // 2**i) % 2) for i in range(steps)]
+
+    barrier = pltpu.get_barrier_semaphore()
+    for other in partners:
+        pl.semaphore_signal(barrier, inc=1, device_id={"seq": other}, device_id_type=MESH)
+    pl.semaphore_wait(barrier, steps)
+
+    lane = lax.broadcasted_iota(jnp.int32, (32, Q), 1)
+    for g in range(groups):
+        turned = jnp.concatenate(
+            [jnp.zeros((Q - RIM, CW), jnp.float32), rim_ref[g].astype(jnp.float32)], axis=0
+        )
+        rim_t[g] = turned.T
+
+    strips = CW // 32
+
+    @pl.loop(0, groups * strips)
+    def _(step):
+        g = step // strips
+        window = pl.ds(pl.multiple_of((step % strips) * 32, 32), 32)
+        par = par_ref[g, window, :]
+        taps = [jnp.broadcast_to(par[:, k : k + 1], (32, Q)) for k in range(KCONV + 1)]
+        earlier = rim_t[g, window, :]
+        old = [pltpu.roll(earlier, d, 1) for d in range(1, KCONV)]
+        for q in range(blocks):
+            now = conv_ref[g, window, q * Q : (q + 1) * Q].astype(jnp.float32)
+            pre = taps[KCONV] + taps[KCONV - 1] * now
+            fresh = [pltpu.roll(now, d, 1) for d in range(1, KCONV)]
+            for d in range(1, KCONV):
+                pre = pre + taps[KCONV - 1 - d] * jnp.where(lane < d, old[d - 1], fresh[d - 1])
+            old = fresh
+            value = 0.5 * pre * (1.0 + jnp.tanh(0.5 * pre))
+            act[g, window, q * Q : (q + 1) * Q] = value.astype(jnp.bfloat16)
+
+    row = lax.broadcasted_iota(jnp.int32, (Q, Q), 0)
+    col = lax.broadcasted_iota(jnp.int32, (Q, Q), 1)
+    causal = row <= col
+    upper = jnp.where(causal, 1.0, 0.0)
+    for g in range(groups):
+        c_ref[g] = act[g, GW + N :, :]
+        heads = head_ref[g]
+        raw = dt_ref[g] + heads[:, 0:1]
+        step_dt = jnp.maximum(raw, 0.0) + jnp.log1p(jnp.exp(-jnp.abs(raw)))
+        dts[g] = step_dt
+        slope = -jnp.exp(heads[:, 1:2]) * step_dt
+        base = jnp.zeros((HG, 1), jnp.float32)
+        for q in range(blocks):
+            tile = slice(q * Q, (q + 1) * Q)
+            cum = jnp.dot(
+                slope[:, tile], upper,
+                precision=lax.Precision.HIGHEST, preferred_element_type=jnp.float32,
+            )
+            cums[g, :, tile] = cum
+            dec_ref[g, :, tile] = jnp.exp(cum + base)
+            base = base + cum[:, Q - 1 :]
+        keep[g] = jnp.broadcast_to(jnp.exp(base), (HG, Q))
+        total[g] = jnp.zeros((GW, N), jnp.float32)
+
+    @pl.loop(0, groups * blocks)
+    def _(unit):
+        g, q = unit // blocks, unit % blocks
+        tile = pl.ds(pl.multiple_of(q * Q, Q), Q)
+        cum = cums[g, :, tile]
+        last = cum[:, Q - 1 :]
+        tail = jnp.exp(last - cum) * dts[g, :, tile]
+        held = jnp.broadcast_to(jnp.exp(last), (HG, Q))
+        states[g, q] = total[g].astype(jnp.bfloat16)
+        b = act[g, GW : GW + N, tile].astype(jnp.float32).T.astype(jnp.bfloat16)
+        for h in range(0, HG, 4):
+            x = act[g, h * P_SIZE : (h + 4) * P_SIZE, tile].astype(jnp.float32)
+            scaled = x.reshape(4, P_SIZE, Q) * tail[h : h + 4][:, None, :]
+            scaled = scaled.reshape(4 * P_SIZE, Q).astype(jnp.bfloat16)
+            fresh = jnp.dot(scaled, b, preferred_element_type=jnp.float32)
+            for i in range(4):
+                span = slice((h + i) * P_SIZE, (h + i + 1) * P_SIZE)
+                total[g, span, :] = (
+                    held[h + i : h + i + 1] * total[g, span, :]
+                    + fresh[i * P_SIZE : (i + 1) * P_SIZE]
+                )
+
+    def inner(unit):
+        g, q = unit // blocks, unit % blocks
+        tile = pl.ds(pl.multiple_of(q * Q, Q), Q)
+        cum = cums[g, :, tile]
+        tall = jnp.concatenate([cum, jnp.zeros((Q - HG, Q), jnp.float32)], axis=0).T
+        dt = dts[g, :, tile]
+        grown = jnp.exp(cum)
+        b = act[g, GW : GW + N, tile].astype(jnp.float32).T.astype(jnp.bfloat16)
+        c = act[g, GW + N :, tile]
+        scores = jnp.where(causal, jnp.dot(b, c, preferred_element_type=jnp.float32), 0.0)
+        for h in range(HG):
+            span = slice(h * P_SIZE, (h + 1) * P_SIZE)
+            x = act[g, span, tile].astype(jnp.float32)
+            across = jnp.dot(states[g, q, span, :], c, preferred_element_type=jnp.float32)
+            spread = cum[h : h + 1] - tall[:, h : h + 1]
+            weights = (scores * jnp.exp(jnp.minimum(spread, 0.0))).astype(jnp.bfloat16)
+            stepped = (x * dt[h : h + 1]).astype(jnp.bfloat16)
+            y = jnp.dot(stepped, weights, preferred_element_type=jnp.float32)
+            part_ref[g, span, tile] = y + grown[h : h + 1] * across + skip_ref[g, h] * x
+
+    def exchange(i):
+        return [
+            pltpu.make_async_remote_copy(
+                src_ref=src.at[i], dst_ref=dst.at[i],
+                send_sem=send_sem.at[i, j], recv_sem=recv_sem.at[i, j],
+                device_id={"seq": partners[i]}, device_id_type=MESH,
+            )
+            for j, (src, dst) in enumerate(((out_state, got_state), (out_keep, got_keep)))
+        ]
+
+    def send(i):
+        out_state[i] = total[...].astype(jnp.bfloat16)
+        out_keep[i] = keep[...]
+        for copy in exchange(i):
+            copy.start()
+
+    before[...] = jnp.zeros_like(before)
+    keep_before[...] = jnp.ones_like(keep_before)
+    units = groups * blocks
+    for i in range(steps):
+        send(i)
+        pl.loop(units * i // steps, units * (i + 1) // steps)(inner)
+        for copy in exchange(i):
+            copy.wait_recv()
+        upper_half = (s // 2**i) % 2
+
+        @pl.when(upper_half == 1)
+        def _():
+            for g in range(groups):
+                for h in range(HG):
+                    span = slice(h * P_SIZE, (h + 1) * P_SIZE)
+                    got = got_state[i, g, span, :].astype(jnp.float32)
+                    before[g, span, :] += keep_before[g, h : h + 1] * got
+                    if i < steps - 1:
+                        total[g, span, :] += keep[g, h : h + 1] * got
+            keep_before[...] = keep_before[...] * got_keep[i]
+
+        if i < steps - 1:
+
+            @pl.when(upper_half == 0)
+            def _():
+                for g in range(groups):
+                    for h in range(HG):
+                        span = slice(h * P_SIZE, (h + 1) * P_SIZE)
+                        got = got_state[i, g, span, :].astype(jnp.float32)
+                        total[g, span, :] = got_keep[i, g, h : h + 1] * total[g, span, :] + got
+
+            keep[...] = keep[...] * got_keep[i]
+
+    in_ref[...] = before[...].astype(jnp.bfloat16)
+    for i in range(steps):
+        for copy in exchange(i):
+            copy.wait_send()
+
+
+def mix(conv, dt, rim, par, heads, skip, ranks):
+    groups, _, rows = conv.shape
+    blocks = rows // Q
+    steps = ranks.bit_length() - 1
+    vmem = pl.BlockSpec(memory_space=pltpu.VMEM)
+    f32, bf16 = jnp.float32, jnp.bfloat16
+    return pl.pallas_call(
+        functools.partial(mix_kernel, ranks),
+        out_shape=(
+            jax.ShapeDtypeStruct((groups, GW, rows), f32),
+            jax.ShapeDtypeStruct((groups, N, rows), bf16),
+            jax.ShapeDtypeStruct((groups, HG, rows), f32),
+            jax.ShapeDtypeStruct((groups, GW, N), bf16),
+        ),
+        in_specs=[vmem] * 5 + [pl.BlockSpec(memory_space=pltpu.SMEM)],
+        out_specs=(vmem,) * 4,
+        scratch_shapes=[
+            pltpu.VMEM((groups, CW, rows), bf16),
+            pltpu.VMEM((groups, CW, Q), f32),
+            pltpu.VMEM((groups, HG, rows), f32),
+            pltpu.VMEM((groups, HG, rows), f32),
+            pltpu.VMEM((groups, blocks, GW, N), bf16),
+            pltpu.VMEM((groups, GW, N), f32),
+            pltpu.VMEM((groups, HG, Q), f32),
+            pltpu.VMEM((groups, GW, N), f32),
+            pltpu.VMEM((groups, HG, Q), f32),
+            pltpu.VMEM((steps, groups, GW, N), bf16),
+            pltpu.VMEM((steps, groups, HG, Q), f32),
+            pltpu.VMEM((steps, groups, GW, N), bf16),
+            pltpu.VMEM((steps, groups, HG, Q), f32),
+            pltpu.SemaphoreType.DMA((steps, 2)),
+            pltpu.SemaphoreType.DMA((steps, 2)),
+        ],
+        compiler_params=pltpu.CompilerParams(
+            collective_id=1, has_side_effects=True, vmem_limit_bytes=56 * 2**20
+        ),
+    )(conv, dt, rim, par, heads, skip)
+
+
+def finish_kernel(part_ref, c_ref, dec_ref, in_ref, gain_ref, out_ref):
+    across = jnp.dot(in_ref[0], c_ref[0], preferred_element_type=jnp.float32)
+    dec = dec_ref[0]
+    grown = across.reshape(HG, P_SIZE, Q) * dec[:, None, :]
+    activity = part_ref[0] + grown.reshape(GW, Q)
+    square = jnp.sum(activity * activity, axis=0, keepdims=True) * (1.0 / GW)
+    normed = (activity * lax.rsqrt(square + epsilon)).T
+    out_ref[...] = (normed * gain_ref[0]).astype(jnp.bfloat16)
+
+
+def finish(part, c, dec, incoming, gain):
+    groups, _, rows = part.shape
+
+    def block(tall, wide=Q):
+        return pl.BlockSpec((1, tall, wide), lambda g, q: (g, 0, q))
+
+    return pl.pallas_call(
+        finish_kernel,
+        grid=(groups, rows // Q),
+        out_shape=jax.ShapeDtypeStruct((rows, groups * GW), jnp.bfloat16),
+        in_specs=[
+            block(GW),
+            block(N),
+            block(HG),
+            pl.BlockSpec((1, GW, N), lambda g, q: (g, 0, 0)),
+            pl.BlockSpec((1, 1, GW), lambda g, q: (g, 0, 0)),
+        ],
+        out_specs=pl.BlockSpec((Q, GW), lambda g, q: (q, g)),
+        compiler_params=pltpu.CompilerParams(vmem_limit_bytes=32 * 2**20),
+    )(part, c, dec, incoming, gain[:, None, :])
+
+
 def shifted(block, axis, distance):
     devices = range(lax.axis_size(axis))
     route = [(i - distance, i) for i in devices if i - distance in devices]
     return lax.ppermute(block, axis, route)
 
 
-def entering(part, axis, combine, identity):
-    place = lax.axis_index(axis)
-    gathered = jax.tree.map(lambda a: lax.all_gather(a, axis), part)
-    state = jax.tree.map(lambda a, e: jnp.zeros_like(a) + jnp.asarray(e, a.dtype), part, identity)
-
-    def one(step, state):
-        return combine(
-            state, jax.tree.map(lambda a: lax.dynamic_index_in_dim(a, step, 0, False), gathered)
-        )
-
-    return lax.fori_loop(0, place, one, state)
-
-
-def combine_states(earlier, later_one):
-    return (earlier[0] * later_one[0], later_one[0][..., None, None] * earlier[1] + later_one[1])
-
-
-def mix_groups(tokens, w_in, conv_w, conv_b, dt_bias, a_log, d_skip, norm_gain):
-    groups = w_in.shape[0]
-    row_count = tokens.shape[0]
-    conv_turned, dt_turned, rim = project(
-        tokens, jnp.swapaxes(w_in, 1, 2), lax.axis_size("chan"), lax.axis_size("seq")
-    )
-    conv_in = jnp.transpose(conv_turned, (2, 0, 1))
-    raw_dt = jnp.transpose(dt_turned, (2, 0, 1))
-    rim_rows = jnp.swapaxes(shifted(rim, "seq", 1)[:, RIM - (KCONV - 1) :], 0, 1)
-    padded = jnp.concatenate([rim_rows, conv_in], axis=0)
-    pre_act = jnp.broadcast_to(conv_b[None], (row_count, groups, CW))
-    for offset in range(KCONV):
-        pre_act = pre_act + conv_w[None, :, offset] * padded[offset : offset + row_count]
-    inputs = jax.nn.silu(pre_act).astype(jnp.bfloat16)
-    block_count = row_count // Q
-    blocked = inputs.reshape(block_count, Q, groups, CW)
-    x_all = blocked[..., :GW].reshape(block_count, Q, groups, HG, P_SIZE)
-    b_all = blocked[..., GW : GW + N]
-    c_all = blocked[..., GW + N :]
-    step_dt = jax.nn.softplus(raw_dt + dt_bias[None]).reshape(block_count, Q, groups, HG)
-    decay_rate = -jnp.exp(a_log)
-    cumulative = jnp.cumsum(decay_rate[None, None] * step_dt, axis=1)
-    causal = lax.broadcasted_iota(jnp.int32, (Q, Q), 0) >= lax.broadcasted_iota(
-        jnp.int32, (Q, Q), 1
-    )
-
-    def local_block(carried, block_in):
-        state_now, factor = carried
-        x_blk, b_blk, c_blk, dt_blk, cum_blk = block_in
-        scores = jnp.einsum("ign,jgn->gij", c_blk, b_blk, preferred_element_type=jnp.float32)
-        cum_cols = jnp.transpose(cum_blk, (1, 2, 0))
-        dt_cols = jnp.transpose(dt_blk, (1, 2, 0))
-        spread = cum_cols[..., :, None] - cum_cols[..., None, :]
-        damping = jnp.where(causal, jnp.exp(jnp.minimum(spread, 0.0)), 0.0)
-        weights = (scores[:, None] * damping * dt_cols[..., None, :]).astype(jnp.bfloat16)
-        partial_y = jnp.einsum(
-            "ghij,jghp->ighp", weights, x_blk, preferred_element_type=jnp.float32
-        )
-        partial_y = partial_y + d_skip[None, :, :, None] * x_blk
-        last_cum = cum_blk[-1]
-        tail_factor = jnp.exp(last_cum[None] - cum_blk) * dt_blk
-        scaled = (x_blk * tail_factor[..., None]).astype(jnp.bfloat16)
-        fresh_state = jnp.einsum(
-            "jghp,jgn->ghpn", scaled, b_blk, preferred_element_type=jnp.float32
-        )
-        keep_blk = jnp.exp(last_cum)
-        carried_next = (keep_blk[..., None, None] * state_now + fresh_state, factor * keep_blk)
-        return (carried_next, (partial_y, fresh_state, keep_blk))
-
-    zero_state = jnp.zeros((groups, HG, P_SIZE, N), jnp.float32)
-    unit_keep = jnp.ones((groups, HG), jnp.float32)
-    (local_end, local_keep), (partial_all, fresh_all, keep_all) = lax.scan(
-        local_block, (zero_state, unit_keep), (x_all, b_all, c_all, step_dt, cumulative)
-    )
-    _, incoming = entering((local_keep, local_end), "seq", combine_states, (unit_keep, zero_state))
-
-    def finish_block(state_now, block_in):
-        partial_y, fresh_state, keep_blk, c_blk, cum_blk = block_in
-        across = jnp.einsum(
-            "ign,ghpn->ighp",
-            c_blk,
-            state_now.astype(jnp.bfloat16),
-            preferred_element_type=jnp.float32,
-        )
-        activity = partial_y + jnp.exp(cum_blk)[..., None] * across
-        flat_act = activity.reshape(Q, groups, GW)
-        inv_rms = lax.rsqrt(jnp.mean(flat_act * flat_act, axis=-1, keepdims=True) + epsilon)
-        normed = (flat_act * inv_rms * norm_gain[None]).astype(jnp.bfloat16)
-        return (keep_blk[..., None, None] * state_now + fresh_state, normed)
-
-    _, outputs = lax.scan(
-        finish_block, incoming, (partial_all, fresh_all, keep_all, c_all, cumulative)
-    )
-    return outputs.reshape(row_count, groups * GW)
-
-
 def per_device(tokens, w_in, conv_w, conv_b, dt_bias, a_log, d_skip, norm_gain):
-    return mix_groups(tokens, w_in, conv_w, conv_b, dt_bias, a_log, d_skip, norm_gain)
+    lines, ranks = lax.axis_size("chan"), lax.axis_size("seq")
+    conv, dt, rim = project(tokens, jnp.swapaxes(w_in, 1, 2), lines, ranks)
+    par = jnp.swapaxes(jnp.concatenate([conv_w, conv_b[:, None]], axis=1), 1, 2)
+    heads = jnp.stack([dt_bias, a_log], axis=2)
+    part, c, dec, incoming = mix(conv, dt, shifted(rim, "seq", 1), par, heads, d_skip, ranks)
+    return finish(part, c, dec, incoming, norm_gain)
 
 
 def solution(mesh):

time: 307 us -> 195 us (0.64)
  Pallas kernels: 116 us -> 180 us
  waiting for transfers between devices: 45.5 us -> 0.01 us
  matrix products: 38.1 us -> 0 us
  other arithmetic: 37.8 us -> 2.14 us
  local copies, waits for them, and re-layouts: 41.5 us -> 7.42 us
  between operations: 13.6 us -> 0.12 us
  blocking collectives: 10.4 us -> 0 us
    pallas_call x0 -> x2, Pallas kernels: none -> 64 us  [the longest x1 55.8 us: mix(): pl.pallas_call(functools.partial(mix_kernel, ranks), out_shape=(jax.Shape...]
    all_gather x1 -> x0, waiting for transfers between devices: 45.5 us -> none  [entering(): gathered = jax.tree.map(lambda a: lax.all_gather(a, axis), part)]
    dot_general x24 -> x0, matrix products: 38.1 us -> none  [the longest x6 19 us: local_block(): jnp.einsum('ghij,jghp->ighp', weights, x_blk, preferred_element_type=jnp....]
    add x13 -> x0, other arithmetic: 18.8 us -> none  [the longest x7 10.1 us: combine_states(): later_one[0][..., None, None] * earlier[1] + later_one[1]]
    dynamic_update_slice x24 -> x0, local copies, waits for them, and re-layouts: 16.6 us -> none  [the longest x12 10.1 us: mix_groups(): lax.scan(finish_block, incoming, (partial_all, fresh_all, keep_all, c_all...]
    convert_element_type x7 -> x0, other arithmetic: 16.2 us -> none  [the longest x1 14.2 us: mix_groups(): inputs = jax.nn.silu(pre_act).astype(jnp.bfloat16)]
    slice x4 -> x0, local copies, waits for them, and re-layouts: 10.7 us -> none  [the longest x2 8.52 us: mix_groups(): x_all = blocked[..., :GW].reshape(block_count, Q, groups, HG, P_SIZE)]
    all_gather x1 -> x0, blocking collectives: 10.4 us -> none  [entering(): gathered = jax.tree.map(lambda a: lax.all_gather(a, axis), part)]
  transfers between devices with their start and end apart: 2 -> 1, of which waited for: 1 -> 0; matrix products, arithmetic and copies ran while one was open for 1% -> 2% of each run, Pallas kernels for 0% -> 0%
where the time goes in v2:
time: 195 us; the launch traced here: 191 us
  Pallas kernels  180 us (92%)
  local copies, waits for them, and re-layouts  7.42 us (4%)
  other arithmetic  2.14 us (1%)
    pallas_call x1, Pallas kernels, project(): pl.pallas_call(functools.partial(project_kernel, lines), out_shape=shapes...  116 us
    pallas_call x1, Pallas kernels, mix(): pl.pallas_call(functools.partial(mix_kernel, ranks), out_shape=(jax.Shape...  55.8 us
    pallas_call x1, Pallas kernels, finish(): pl.pallas_call(finish_kernel, grid=(groups, rows // Q), out_shape=jax.Sha...  8.14 us
    unnamed x21, local copies, waits for them, and re-layouts  6.8 us
  transfers between devices with their start and end apart: 1, of which 0 were waited for; matrix products, arithmetic and copies ran while one was open for 2% of the time, Pallas kernels for 0%

profile of v2, /device:TPU:7, one launch (start us, length us, event | category | flops | bytes accessed | tf_op | source)
XLA Modules:
  0.0 190.8 jit_solution(17015462323672324555)
XLA Ops:
  0.0 0.0 copy-start.5
  0.0 115.8 %shard_map.82 = (bf16[2,1280,768]{2,1,0:T(8,128)(2,1)}, f32[2,16,768]{2,1,0:T(8,128)}, bf16[2,16,1280]{2,1,0:T(8,128)(2,1)}) custom-call(bf16[768,1024]{1,0:T(8,128)(2,1)} %tok_ref.1, bf16[2,1296,512]{2,1,0:T(8,128)(2,1)} %bitcast.6), custom_call_target="tpu_custom_call" | custom-call | tf_op jit(solution)/shard_map/pallas_call | solution.py:207
  115.8 0.0 copy-start.6
  115.8 0.0 copy-start.8
  115.8 0.0 copy-start.9
  115.8 0.0 copy-start.7
  115.8 1.4 collective-permute-start
  117.3 0.0 copy-done.5
  117.3 0.4 copy.21
  117.7 0.0 copy-done.6
  117.7 0.4 copy.22
  118.2 0.0 copy-done.8
  118.2 0.1 copy.23
  118.3 0.0 copy-done.9
  118.3 0.1 copy.24
  118.3 0.0 copy-done.7
  118.4 1.5 maximum_bitcast_fusion.par_ref
  119.8 0.7 pad_maximum_fusion.head_ref
  120.5 0.0 collective-permute-done.rim_ref
  120.5 0.0 copy-start.4
  120.5 0.6 copy-done.4
  121.1 55.8 %shard_map.83 = (f32[2,1024,768]{2,1,0:T(8,128)}, bf16[2,128,768]{2,1,0:T(8,128)(2,1)}, f32[2,16,768]{2,1,0:T(8,128)}, bf16[2,1024,128]{2,1,0:T(8,128)(2,1)}) custom-call(bf16[2,1280,768]{2,1,0:T(8,128)(2,1)} %get-tuple-element.12.conv_ref, f32[2,16,768]{2,1,0:T(8,128)} %get-tuple-element.13.dt_ref, bf16[2,16,1280]{2,1,0:T(8,128)(2,1)} %copy-done.4, ...), custom_call_target="tpu_custom_call" | custom-call | tf_op jit(solution)/shard_map/pallas_call | solution.py:406
  177.0 0.0 copy-start
  177.0 2.8 %copy-done = f32[2,1024,768]{2,1,0:T(8,128)S(1)} copy-done((f32[2,1024,768]{2,1,0:T(8,128)S(1)}, f32[2,1024,768]{2,1,0:T(8,128)}, u32[]{:S(2)}) %copy-start) | copy-done | bytes 6291480
  179.8 0.0 copy-start.1
  179.8 1.0 copy-done.1
  180.8 0.0 copy-start.2
  180.8 1.0 copy-done.2
  181.8 0.0 copy-start.3
  181.8 0.9 copy-done.3
  182.7 8.1 %shard_map.84 = bf16[768,2048]{1,0:T(8,128)(2,1)} custom-call(f32[2,1024,768]{2,1,0:T(8,128)S(1)} %copy-done, bf16[2,128,768]{2,1,0:T(8,128)(2,1)S(1)} %copy-done.2, f32[2,16,768]{2,1,0:T(8,128)S(1)} %copy-done.3, bf16[2,1024,128]{2,1,0:T(8,128)(2,1)S(1)} %copy-done.1, f32[2,1,1024]{2,1,0:T(1,128)S(1)} %broadcast_in_dim.7.gain_ref), custom_call_target="tpu_custom_call" | custom-call | tf_op jit(solution)/shard_map/pallas_call | solution.py:455
  (1 shorter events, 0.0 us)
Async XLA Ops:
  0.0 117.3 %copy-start.5 = (f32[2,4,1280]{2,1,0:T(4,128)S(1)}, f32[2,4,1280]{2,1,0:T(4,128)}, u32[]{:S(2)}) copy-start(f32[2,4,1280]{2,1,0:T(4,128)} %param.10) | copy-start | bytes 122884
  115.8 1.9 %copy-start.6 = (f32[2,1280]{1,0:T(2,128)S(1)}, f32[2,1280]{1,0:T(2,128)}, u32[]{:S(2)}) copy-start(f32[2,1280]{1,0:T(2,128)} %param.11) | copy-start | bytes 30724
  115.8 2.4 %copy-start.8 = (f32[2,16]{1,0:T(2,128)S(1)}, f32[2,16]{1,0:T(2,128)}, u32[]{:S(2)}) copy-start(f32[2,16]{1,0:T(2,128)} %param.12) | copy-start | bytes 388
  115.8 2.5 %copy-start.9 = (f32[2,16]{1,0:T(2,128)S(1)}, f32[2,16]{1,0:T(2,128)}, u32[]{:S(2)}) copy-start(f32[2,16]{1,0:T(2,128)} %param.13) | copy-start | bytes 388
  115.8 2.5 %copy-start.7 = (f32[2,1024]{1,0:T(2,128)S(1)}, f32[2,1024]{1,0:T(2,128)}, u32[]{:S(2)}) copy-start(f32[2,1024]{1,0:T(2,128)} %param.15) | copy-start | bytes 24580
  115.8 4.7 %collective-permute-start = (bf16[2,16,1280]{2,1,0:T(8,128)(2,1)}, bf16[2,16,1280]{2,1,0:T(8,128)(2,1)S(1)}, u32[]{:S(2)}, u32[]{:S(2)}) collective-permute-start(bf16[2,16,1280]{2,1,0:T(8,128)(2,1)} %get-tuple-element.14), channel_id=1, source_target_pairs={{0,4},{4,8},{8,12},{12,16},{16,20},{20,24},{24,28},{1,5},{5,9},{9,... | collective-permute-start | bytes 245768 | tf_op jit(solution)/shard_map/ppermute | solution.py:474
  120.5 0.6 copy-start.4
  177.0 2.8 %copy-start = (f32[2,1024,768]{2,1,0:T(8,128)S(1)}, f32[2,1024,768]{2,1,0:T(8,128)}, u32[]{:S(2)}) copy-start(f32[2,1024,768]{2,1,0:T(8,128)} %get-tuple-element.15.part_ref) | copy-start | bytes 18874372
  179.8 1.0 copy-start.1
  180.8 1.0 copy-start.2
  181.8 0.9 copy-start.3

commit v3 on v2

--- a/solution.py
+++ b/solution.py
@@ -123,60 +123,66 @@
         if k < lines - 1:
             tok_sends(k, part, start)
 
+    acc[...] = jnp.zeros_like(acc)
+    tiles = 3
+    tall = cols // tiles
+
+    def product(shard, first, last):
+        @pl.loop(first * groups * tiles, last * groups * tiles)
+        def _(step):
+            part = step // (groups * tiles)
+            g = (step // tiles) % groups
+            window = pl.ds(pl.multiple_of((step % tiles) * tall, 16), tall)
+            span = pl.ds(pl.multiple_of(part * half, 128), half)
+            total = None
+            for i in range(ratio):
+                term = lax.dot_general(
+                    w_all[shard * ratio + i, g, window, :],
+                    tok_all[shard, span, i * depth : (i + 1) * depth],
+                    (((1,), (1,)), ((), ())),
+                    preferred_element_type=jnp.float32,
+                )
+                total = term if total is None else total + term
+            acc[g, window, span] += total
+
     relay(1, 0)
     near_weights(0)
     relay(1, 1)
-    if lines > 2:
-        relay(2, 0)
+    relay(2, 0)
     near_weights(1)
-    if lines > 2:
-        relay(2, 1)
-    far_weights(0)
-    far_weights(1)
-    for k in range(3, lines - 1):
-        relay(k, 0)
-        relay(k, 1)
-    for shard in (sib, sib + xs - s, sib + ys - s, sib + diag - s):
+    relay(2, 1)
+    for shard in (sib, sib + xs - s, sib + ys - s):
         for g in range(groups):
             w_copy(shard, g, w_own.at[2, g], sib, False).wait_recv()
     own_tok.wait()
     own_w.wait()
-
-    tiles = 3
-    tall = cols // tiles
-
-    def product(shard, first):
-        @pl.loop(0, groups * tiles)
-        def _(step):
-            g = step // tiles
-            window = pl.ds(pl.multiple_of((step % tiles) * tall, 16), tall)
-            total = None
-            for i in range(ratio):
-                term = lax.dot_general(
-                    w_all[shard * ratio + i, g, window, :],
-                    tok_all[shard, :, i * depth : (i + 1) * depth],
-                    (((1,), (1,)), ((), ())),
-                    preferred_element_type=jnp.float32,
-                )
-                total = term if total is None else total + term
-            if first:
-                acc[g, window, :] = total
-            else:
-                acc[g, window, :] += total
-
-    product(c, True)
-    for k in range(1, lines):
-        if k >= 3 and k == lines - 1:
-            tok_arrive(k, 0)
-            tok_arrive(k, 1)
-
-        @pl.when(c - k >= 0)
-        def _():
-            product(c - k, False)
-
-        @pl.when(c + k < lines)
-        def _():
-            product(c + k, False)
+    far = diag // ratio
+
+    @pl.loop(0, lines)
+    def _(shard):
+        @pl.when((shard != far) & (shard - c < 3) & (c - shard < 3))
+        def _():
+            product(shard, 0, 2)
+
+    far_weights(0)
+    far_weights(1)
+    for g in range(groups):
+        w_copy(sib + diag - s, g, w_own.at[2, g], sib, False).wait_recv()
+
+    @pl.when((far - c < 3) & (c - far < 3))
+    def _():
+        product(far, 0, 2)
+
+    for part in range(2):
+        tok_arrive(3, part)
+
+        @pl.when(c == 0)
+        def _():
+            product(3, part, part + 1)
+
+        @pl.when(c == 3)
+        def _():
+            product(0, part, part + 1)
 
     for g in range(groups):
         conv_ref[g] = acc[g, :CW, :].astype(jnp.bfloat16)
@@ -202,7 +208,7 @@
         jax.ShapeDtypeStruct((groups, cols - CW, rows), jnp.float32),
         jax.ShapeDtypeStruct((groups, RIM, CW), jnp.bfloat16),
     )
-    if ranks == 8 and groups == 2 and lines > 1:
+    if ranks == 8 and groups == 2 and lines == 4:
         dma = pltpu.SemaphoreType.DMA
         return pl.pallas_call(
             functools.partial(project_kernel, lines),
@@ -233,8 +239,9 @@
 
 
 def mix_kernel(
-    ranks, conv_ref, dt_ref, rim_ref, par_ref, head_ref, skip_ref,
-    part_ref, c_ref, dec_ref, in_ref,
+    ranks, conv_ref, dt_ref, rim_ref, tap_ref, shift_ref, head_ref, skip_ref,
+    part_out, c_out, dec_out, in_out,
+    part_ref, dec_ref, in_ref, out_sem, unit_sem, par_ref,
     act, rim_t, dts, cums, states, total, keep, before, keep_before,
     out_state, out_keep, got_state, got_keep, send_sem, recv_sem,
 ):
@@ -255,6 +262,10 @@
             [jnp.zeros((Q - RIM, CW), jnp.float32), rim_ref[g].astype(jnp.float32)], axis=0
         )
         rim_t[g] = turned.T
+        taps = jnp.concatenate(
+            [tap_ref[g], shift_ref[g : g + 1], jnp.zeros((Q - KCONV - 1, CW), jnp.float32)], axis=0
+        )
+        par_ref[g] = taps.T
 
     strips = CW // 32
 
@@ -281,7 +292,6 @@
     causal = row <= col
     upper = jnp.where(causal, 1.0, 0.0)
     for g in range(groups):
-        c_ref[g] = act[g, GW + N :, :]
         heads = head_ref[g]
         raw = dt_ref[g] + heads[:, 0:1]
         step_dt = jnp.maximum(raw, 0.0) + jnp.log1p(jnp.exp(-jnp.abs(raw)))
@@ -299,6 +309,13 @@
             base = base + cum[:, Q - 1 :]
         keep[g] = jnp.broadcast_to(jnp.exp(base), (HG, Q))
         total[g] = jnp.zeros((GW, N), jnp.float32)
+
+    early = [
+        pltpu.make_async_copy(act.at[:, pl.ds(GW + N, N)], c_out, out_sem.at[0]),
+        pltpu.make_async_copy(dec_ref, dec_out, out_sem.at[1]),
+    ]
+    for copy in early:
+        copy.start()
 
     @pl.loop(0, groups * blocks)
     def _(unit):
@@ -322,6 +339,13 @@
                     + fresh[i * P_SIZE : (i + 1) * P_SIZE]
                 )
 
+    def leave(unit):
+        g, q = unit // blocks, unit % blocks
+        tile = pl.ds(pl.multiple_of(q * Q, Q), Q)
+        return pltpu.make_async_copy(
+            part_ref.at[g, :, tile], part_out.at[g, :, tile], unit_sem.at[unit]
+        )
+
     def inner(unit):
         g, q = unit // blocks, unit % blocks
         tile = pl.ds(pl.multiple_of(q * Q, Q), Q)
@@ -335,12 +359,16 @@
         for h in range(HG):
             span = slice(h * P_SIZE, (h + 1) * P_SIZE)
             x = act[g, span, tile].astype(jnp.float32)
-            across = jnp.dot(states[g, q, span, :], c, preferred_element_type=jnp.float32)
+            if h % 4 == 0:
+                wide = slice(h * P_SIZE, (h + 4) * P_SIZE)
+                four = jnp.dot(states[g, q, wide, :], c, preferred_element_type=jnp.float32)
+            across = four[(h % 4) * P_SIZE : (h % 4 + 1) * P_SIZE]
             spread = cum[h : h + 1] - tall[:, h : h + 1]
             weights = (scores * jnp.exp(jnp.minimum(spread, 0.0))).astype(jnp.bfloat16)
             stepped = (x * dt[h : h + 1]).astype(jnp.bfloat16)
             y = jnp.dot(stepped, weights, preferred_element_type=jnp.float32)
             part_ref[g, span, tile] = y + grown[h : h + 1] * across + skip_ref[g, h] * x
+        leave(unit).start()
 
     def exchange(i):
         return [
@@ -392,12 +420,22 @@
             keep[...] = keep[...] * got_keep[i]
 
     in_ref[...] = before[...].astype(jnp.bfloat16)
+    late = pltpu.make_async_copy(in_ref, in_out, out_sem.at[2])
+    late.start()
+    for copy in early:
+        copy.wait()
+
+    @pl.loop(0, units)
+    def _(unit):
+        leave(unit).wait()
+
+    late.wait()
     for i in range(steps):
         for copy in exchange(i):
             copy.wait_send()
 
 
-def mix(conv, dt, rim, par, heads, skip, ranks):
+def mix(conv, dt, rim, taps, shift, heads, skip, ranks):
     groups, _, rows = conv.shape
     blocks = rows // Q
     steps = ranks.bit_length() - 1
@@ -411,9 +449,15 @@
             jax.ShapeDtypeStruct((groups, HG, rows), f32),
             jax.ShapeDtypeStruct((groups, GW, N), bf16),
         ),
-        in_specs=[vmem] * 5 + [pl.BlockSpec(memory_space=pltpu.SMEM)],
-        out_specs=(vmem,) * 4,
+        in_specs=[vmem] * 6 + [pl.BlockSpec(memory_space=pltpu.SMEM)],
+        out_specs=(pl.BlockSpec(memory_space=pl.ANY),) * 4,
         scratch_shapes=[
+            pltpu.VMEM((groups, GW, rows), f32),
+            pltpu.VMEM((groups, HG, rows), f32),
+            pltpu.VMEM((groups, GW, N), bf16),
+            pltpu.SemaphoreType.DMA((3,)),
+            pltpu.SemaphoreType.DMA((groups * blocks,)),
+            pltpu.VMEM((groups, CW, Q), f32),
             pltpu.VMEM((groups, CW, rows), bf16),
             pltpu.VMEM((groups, CW, Q), f32),
             pltpu.VMEM((groups, HG, rows), f32),
@@ -433,7 +477,7 @@
         compiler_params=pltpu.CompilerParams(
             collective_id=1, has_side_effects=True, vmem_limit_bytes=56 * 2**20
         ),
-    )(conv, dt, rim, par, heads, skip)
+    )(conv, dt, rim, taps, shift, heads, skip)
 
 
 def finish_kernel(part_ref, c_ref, dec_ref, in_ref, gain_ref, out_ref):
@@ -477,9 +521,9 @@
 def per_device(tokens, w_in, conv_w, conv_b, dt_bias, a_log, d_skip, norm_gain):
     lines, ranks = lax.axis_size("chan"), lax.axis_size("seq")
     conv, dt, rim = project(tokens, jnp.swapaxes(w_in, 1, 2), lines, ranks)
-    par = jnp.swapaxes(jnp.concatenate([conv_w, conv_b[:, None]], axis=1), 1, 2)
     heads = jnp.stack([dt_bias, a_log], axis=2)
-    part, c, dec, incoming = mix(conv, dt, shifted(rim, "seq", 1), par, heads, d_skip, ranks)
+    rim = shifted(rim, "seq", 1)
+    part, c, dec, incoming = mix(conv, dt, rim, conv_w, conv_b, heads, d_skip, ranks)
     return finish(part, c, dec, incoming, norm_gain)
 
 

time: 195 us -> 188 us (0.964)
  the two profiles are of different devices: /device:TPU:7 before, /device:TPU:0 now
where the time goes in v3:
time: 188 us; the launch traced here: 187 us
  Pallas kernels  178 us (95%)
  local copies, waits for them, and re-layouts  6.54 us (3%)
  starting transfers between devices  2.03 us (1%)
    pallas_call x1, Pallas kernels, project(): pl.pallas_call(functools.partial(project_kernel, lines), out_shape=shapes...  114 us
    pallas_call x1, Pallas kernels, mix(): pl.pallas_call(functools.partial(mix_kernel, ranks), out_shape=(jax.Shape...  56 us
    pallas_call x1, Pallas kernels, finish(): pl.pallas_call(finish_kernel, grid=(groups, rows // Q), out_shape=jax.Sha...  8.15 us
    unnamed x16, local copies, waits for them, and re-layouts  6.35 us
  transfers between devices with their start and end apart: 1, of which 1 were waited for; matrix products, arithmetic and copies ran while one was open for 0% of the time, Pallas kernels for 0%

profile of v3, /device:TPU:0, one launch (start us, length us, event | category | flops | bytes accessed | tf_op | source)
XLA Modules:
  0.0 187.3 jit_solution(9488182276794563599)
XLA Ops:
  0.0 0.0 copy-start.6
  0.0 0.0 copy-start.7
  0.0 0.0 copy-start.5
  0.0 113.5 %shard_map.82 = (bf16[2,1280,768]{2,1,0:T(8,128)(2,1)}, f32[2,16,768]{2,1,0:T(8,128)}, bf16[2,16,1280]{2,1,0:T(8,128)(2,1)}) custom-call(bf16[768,1024]{1,0:T(8,128)(2,1)} %tok_ref.1, bf16[2,1296,512]{2,1,0:T(8,128)(2,1)} %bitcast.3), custom_call_target="tpu_custom_call" | custom-call | tf_op jit(solution)/shard_map/pallas_call | solution.py:213
  113.6 2.0 %collective-permute-start = (bf16[2,16,1280]{2,1,0:T(8,128)(2,1)}, bf16[2,16,1280]{2,1,0:T(8,128)(2,1)S(1)}, u32[]{:S(2)}, u32[]{:S(2)}) collective-permute-start(bf16[2,16,1280]{2,1,0:T(8,128)(2,1)} %get-tuple-element.14), channel_id=1, source_target_pairs={{0,4},{4,8},{8,12},{12,16},{16,20},{20,24},{24,28},{1,5},{5,9},{9,... | collective-permute-start | bytes 245768 | tf_op jit(solution)/shard_map/ppermute | solution.py:518
  115.6 0.0 copy-done.6
  115.6 0.1 copy.14
  115.7 0.0 copy-done.7
  115.7 0.1 copy.15
  115.8 0.0 copy-done.5
  115.8 0.7 pad_maximum_fusion.head_ref
  116.5 0.2 collective-permute-done.rim_ref
  116.7 0.0 copy-start.4
  116.7 0.6 copy-done.4
  117.3 56.0 %shard_map.83 = (f32[2,1024,768]{2,1,0:T(8,128)}, bf16[2,128,768]{2,1,0:T(8,128)(2,1)}, f32[2,16,768]{2,1,0:T(8,128)}, bf16[2,1024,128]{2,1,0:T(8,128)(2,1)}) custom-call(bf16[2,1280,768]{2,1,0:T(8,128)(2,1)} %get-tuple-element.12.conv_ref, f32[2,16,768]{2,1,0:T(8,128)} %get-tuple-element.13.dt_ref, bf16[2,16,1280]{2,1,0:T(8,128)(2,1)} %copy-done.4, ...), custom_call_target="tpu_custom_call" | custom-call | tf_op jit(solution)/shard_map/pallas_call | solution.py:444
  173.4 0.0 copy-start
  173.4 2.8 %copy-done = f32[2,1024,768]{2,1,0:T(8,128)S(1)} copy-done((f32[2,1024,768]{2,1,0:T(8,128)S(1)}, f32[2,1024,768]{2,1,0:T(8,128)}, u32[]{:S(2)}) %copy-start) | copy-done | bytes 6291480
  176.2 0.0 copy-start.1
  176.2 1.0 copy-done.1
  177.2 0.0 copy-start.2
  177.2 1.0 copy-done.2
  178.2 0.0 copy-start.3
  178.2 0.9 copy-done.3
  179.1 8.1 %shard_map.84 = bf16[768,2048]{1,0:T(8,128)(2,1)} custom-call(f32[2,1024,768]{2,1,0:T(8,128)S(1)} %copy-done, bf16[2,128,768]{2,1,0:T(8,128)(2,1)S(1)} %copy-done.2, f32[2,16,768]{2,1,0:T(8,128)S(1)} %copy-done.3, bf16[2,1024,128]{2,1,0:T(8,128)(2,1)S(1)} %copy-done.1, f32[2,1,1024]{2,1,0:T(1,128)S(1)} %broadcast_in_dim.3.gain_ref), custom_call_target="tpu_custom_call" | custom-call | tf_op jit(solution)/shard_map/pallas_call | solution.py:499
  (1 shorter events, 0.0 us)
Async XLA Ops:
  0.0 115.6 %copy-start.6 = (f32[2,16]{1,0:T(2,128)S(1)}, f32[2,16]{1,0:T(2,128)}, u32[]{:S(2)}) copy-start(f32[2,16]{1,0:T(2,128)} %param.12) | copy-start | bytes 388
  0.0 115.7 %copy-start.7 = (f32[2,16]{1,0:T(2,128)S(1)}, f32[2,16]{1,0:T(2,128)}, u32[]{:S(2)}) copy-start(f32[2,16]{1,0:T(2,128)} %param.13) | copy-start | bytes 388
  0.0 115.8 %copy-start.5 = (f32[2,1024]{1,0:T(2,128)S(1)}, f32[2,1024]{1,0:T(2,128)}, u32[]{:S(2)}) copy-start(f32[2,1024]{1,0:T(2,128)} %param.15) | copy-start | bytes 24580
  113.6 3.1 %collective-permute-start = (bf16[2,16,1280]{2,1,0:T(8,128)(2,1)}, bf16[2,16,1280]{2,1,0:T(8,128)(2,1)S(1)}, u32[]{:S(2)}, u32[]{:S(2)}) collective-permute-start(bf16[2,16,1280]{2,1,0:T(8,128)(2,1)} %get-tuple-element.14), channel_id=1, source_target_pairs={{0,4},{4,8},{8,12},{12,16},{16,20},{20,24},{24,28},{1,5},{5,9},{9,... | collective-permute-start | bytes 245768 | tf_op jit(solution)/shard_map/ppermute | solution.py:518
  116.7 0.6 copy-start.4
  173.4 2.8 %copy-start = (f32[2,1024,768]{2,1,0:T(8,128)S(1)}, f32[2,1024,768]{2,1,0:T(8,128)}, u32[]{:S(2)}) copy-start(f32[2,1024,768]{2,1,0:T(8,128)} %get-tuple-element.15.part_ref) | copy-start | bytes 18874372
  176.2 1.0 copy-start.1
  177.2 1.0 copy-start.2
  178.2 0.9 copy-start.3

commit v4 on v3

--- a/solution.py
+++ b/solution.py
@@ -17,6 +17,7 @@
 MESH = pl.DeviceIdType.MESH
 
 epsilon = 1e-05
+LOG2_E = 1.4426950408889634
 
 
 def project_kernel(
@@ -350,9 +351,10 @@
         g, q = unit // blocks, unit % blocks
         tile = pl.ds(pl.multiple_of(q * Q, Q), Q)
         cum = cums[g, :, tile]
+        grown = jnp.exp(cum)
+        cum = cum * LOG2_E
         tall = jnp.concatenate([cum, jnp.zeros((Q - HG, Q), jnp.float32)], axis=0).T
         dt = dts[g, :, tile]
-        grown = jnp.exp(cum)
         b = act[g, GW : GW + N, tile].astype(jnp.float32).T.astype(jnp.bfloat16)
         c = act[g, GW + N :, tile]
         scores = jnp.where(causal, jnp.dot(b, c, preferred_element_type=jnp.float32), 0.0)
@@ -364,7 +366,7 @@
                 four = jnp.dot(states[g, q, wide, :], c, preferred_element_type=jnp.float32)
             across = four[(h % 4) * P_SIZE : (h % 4 + 1) * P_SIZE]
             spread = cum[h : h + 1] - tall[:, h : h + 1]
-            weights = (scores * jnp.exp(jnp.minimum(spread, 0.0))).astype(jnp.bfloat16)
+            weights = (scores * jnp.exp2(jnp.minimum(spread, 0.0))).astype(jnp.bfloat16)
             stepped = (x * dt[h : h + 1]).astype(jnp.bfloat16)
             y = jnp.dot(stepped, weights, preferred_element_type=jnp.float32)
             part_ref[g, span, tile] = y + grown[h : h + 1] * across + skip_ref[g, h] * x
@@ -389,9 +391,10 @@
     before[...] = jnp.zeros_like(before)
     keep_before[...] = jnp.ones_like(keep_before)
     units = groups * blocks
+    cuts = [0] + [1 + (units - 1) * i // (steps - 1) for i in range(steps)]
     for i in range(steps):
         send(i)
-        pl.loop(units * i // steps, units * (i + 1) // steps)(inner)
+        pl.loop(cuts[i], cuts[i + 1])(inner)
         for copy in exchange(i):
             copy.wait_recv()
         upper_half = (s // 2**i) % 2
@@ -508,7 +511,7 @@
             pl.BlockSpec((1, 1, GW), lambda g, q: (g, 0, 0)),
         ],
         out_specs=pl.BlockSpec((Q, GW), lambda g, q: (q, g)),
-        compiler_params=pltpu.CompilerParams(vmem_limit_bytes=32 * 2**20),
+        compiler_params=pltpu.CompilerParams(vmem_limit_bytes=60 * 2**20),
     )(part, c, dec, incoming, gain[:, None, :])
 
 

time: 188 us -> 186 us (0.989)
  the two profiles are of different devices: /device:TPU:0 before, /device:TPU:7 now
where the time goes in v4:
time: 186 us; the launch traced here: 183 us
  Pallas kernels  179 us (96%)
    pallas_call x1, Pallas kernels, project(): pl.pallas_call(functools.partial(project_kernel, lines), out_shape=shapes...  112 us
    pallas_call x1, Pallas kernels, mix(): pl.pallas_call(functools.partial(mix_kernel, ranks), out_shape=(jax.Shape...  55.3 us
    pallas_call x1, Pallas kernels, finish(): pl.pallas_call(finish_kernel, grid=(groups, rows // Q), out_shape=jax.Sha...  11.6 us
  transfers between devices with their start and end apart: 1, of which 1 were waited for; matrix products, arithmetic and copies ran while one was open for 1% of the time, Pallas kernels for 0%

profile of v4, /device:TPU:7, one launch (start us, length us, event | category | flops | bytes accessed | tf_op | source)
XLA Modules:
  0.0 183.3 jit_solution(11608662071928258397)
XLA Ops:
  0.0 0.0 copy-start.2
  0.0 0.0 copy-start.3
  0.0 0.0 copy-start.1
  0.0 112.4 %shard_map.82 = (bf16[2,1280,768]{2,1,0:T(8,128)(2,1)}, f32[2,16,768]{2,1,0:T(8,128)}, bf16[2,16,1280]{2,1,0:T(8,128)(2,1)}) custom-call(bf16[768,1024]{1,0:T(8,128)(2,1)} %tok_ref.1, bf16[2,1296,512]{2,1,0:T(8,128)(2,1)} %bitcast.3), custom_call_target="tpu_custom_call" | custom-call | tf_op jit(solution)/shard_map/pallas_call | solution.py:214
  112.4 1.3 collective-permute-start
  113.7 0.0 copy-done.2
  113.7 0.1 copy.14
  113.8 0.0 copy-done.3
  113.8 0.1 copy.15
  113.9 0.0 copy-done.1
  113.9 0.6 broadcast_in_dim.3.gain_ref
  114.5 0.7 pad_maximum_fusion.head_ref
  115.2 0.6 collective-permute-done.rim_ref
  115.8 0.0 copy-start
  115.8 0.6 copy-done
  116.4 55.3 %shard_map.83 = (f32[2,1024,768]{2,1,0:T(8,128)}, bf16[2,128,768]{2,1,0:T(8,128)(2,1)}, f32[2,16,768]{2,1,0:T(8,128)}, bf16[2,1024,128]{2,1,0:T(8,128)(2,1)}) custom-call(bf16[2,1280,768]{2,1,0:T(8,128)(2,1)} %get-tuple-element.12.conv_ref, f32[2,16,768]{2,1,0:T(8,128)} %get-tuple-element.13.dt_ref, bf16[2,16,1280]{2,1,0:T(8,128)(2,1)} %copy-done, ...), custom_call_target="tpu_custom_call" | custom-call | tf_op jit(solution)/shard_map/pallas_call | solution.py:447
  171.8 11.6 %shard_map.84 = bf16[768,2048]{1,0:T(8,128)(2,1)} custom-call(f32[2,1024,768]{2,1,0:T(8,128)} %get-tuple-element.15.part_ref, bf16[2,128,768]{2,1,0:T(8,128)(2,1)} %get-tuple-element.16.c_ref, f32[2,16,768]{2,1,0:T(8,128)} %get-tuple-element.17.dec_ref, bf16[2,1024,128]{2,1,0:T(8,128)(2,1)} %get-tuple-element.18.in_ref, f32[2,1,1024]{2,1,0:T(1,128)} %broadcast_in_dim.3.gain_ref), custom_call_target="tpu_custom_call" | custom-call | tf_op jit(solution)/shard_map/pallas_call | solution.py:502
Async XLA Ops:
  0.0 113.7 %copy-start.2 = (f32[2,16]{1,0:T(2,128)S(1)}, f32[2,16]{1,0:T(2,128)}, u32[]{:S(2)}) copy-start(f32[2,16]{1,0:T(2,128)} %param.12) | copy-start | bytes 388
  0.0 113.8 %copy-start.3 = (f32[2,16]{1,0:T(2,128)S(1)}, f32[2,16]{1,0:T(2,128)}, u32[]{:S(2)}) copy-start(f32[2,16]{1,0:T(2,128)} %param.13) | copy-start | bytes 388
  0.0 113.9 %copy-start.1 = (f32[2,1024]{1,0:T(2,128)S(1)}, f32[2,1024]{1,0:T(2,128)}, u32[]{:S(2)}) copy-start(f32[2,1024]{1,0:T(2,128)} %param.15) | copy-start | bytes 24580
  112.4 3.4 %collective-permute-start = (bf16[2,16,1280]{2,1,0:T(8,128)(2,1)}, bf16[2,16,1280]{2,1,0:T(8,128)(2,1)S(1)}, u32[]{:S(2)}, u32[]{:S(2)}) collective-permute-start(bf16[2,16,1280]{2,1,0:T(8,128)(2,1)} %get-tuple-element.14), channel_id=1, source_target_pairs={{0,4},{4,8},{8,12},{12,16},{16,20},{20,24},{24,28},{1,5},{5,9},{9,... | collective-permute-start | bytes 245768 | tf_op jit(solution)/shard_map/ppermute | solution.py:521
  115.8 0.6 copy-start
